TPU v7x, 32 devices: a whole 2x2x4 slice. The times are simulated.
32 devices in a mesh: wide: 8 (over y, x, core), narrow: 4 (over z).
Axes of the slice: x: 2, y: 2, z: 4, core: 2. Of those that a mesh axis runs over, the one named last changes fastest.
Arguments:
- tokens: bfloat16 [16384, 1152], P(('wide', 'narrow')), may hold values from -6 to 6
- condition: bfloat16 [5, 1152], replicated, may hold values from -6 to 6
- q_weight: bfloat16 [1152, 1152], P(None, 'narrow'), may hold values from -0.1875 to 0.1875
- q_bias: bfloat16 [1152], P('narrow'), may hold values from -4 to 4
- k_weight: bfloat16 [1152, 1152], P(None, 'narrow'), may hold values from -0.1875 to 0.1875
- v_weight: bfloat16 [1152, 1152], P(None, 'narrow'), may hold values from -0.1875 to 0.1875
- v_bias: bfloat16 [1152], P('narrow'), may hold values from -4 to 4
- o_weight: bfloat16 [1152, 1152], P('narrow'), may hold values from -1.5 to 1.5
- o_bias: bfloat16 [1152], replicated, may hold values from -4 to 4
- up_weight: bfloat16 [1152, 4608], P(None, 'narrow'), may hold values from -0.1875 to 0.1875
- up_bias: bfloat16 [4608], P('narrow'), may hold values from -6 to 6
- down_weight: bfloat16 [4608, 1152], P('narrow'), may hold values from -0.09375 to 0.09375
- down_bias: bfloat16 [1152], replicated, may hold values from -4 to 4
- ada_weight: bfloat16 [1152, 6, 1152], P(None, None, 'narrow'), may hold values from -0.1875 to 0.1875
- ada_bias: bfloat16 [6, 1152], P(None, 'narrow'), may hold values from -6 to 6
- out_grad: bfloat16 [16384, 1152], P(('wide', 'narrow')), may hold values from -6 to 6
- slot_clip: int32 [16], P('wide'), may hold values from 0 to 4, as said below
- clip_patches: int32 [5], replicated, may hold values from 256 to 1024, as said below
Outputs:
- block_out: bfloat16 [16384, 1152], P(('wide', 'narrow'))
- grad_tokens: float32 [16384, 1152], P(('wide', 'narrow'))
- grad_condition: float32 [5, 1152], replicated
- grad_q_weight: float32 [1152, 1152], P(None, 'narrow')
- grad_q_bias: float32 [1152], P('narrow')
- grad_k_weight: float32 [1152, 1152], P(None, 'narrow')
- grad_v_weight: float32 [1152, 1152], P(None, 'narrow')
- grad_v_bias: float32 [1152], P('narrow')
- grad_o_weight: float32 [1152, 1152], P('narrow')
- grad_o_bias: float32 [1152], replicated
- grad_up_weight: float32 [1152, 4608], P(None, 'narrow')
- grad_up_bias: float32 [4608], P('narrow')
- grad_down_weight: float32 [4608, 1152], P('narrow')
- grad_down_bias: float32 [1152], replicated
- grad_ada_weight: float32 [1152, 6, 1152], P(None, None, 'narrow')
- grad_ada_bias: float32 [6, 1152], P(None, 'narrow')
Inputs may be any that keep to these rules, and one draw needn't show every extreme that they name: Slot s holds rows s * 1024 to (s + 1) * 1024 - 1 of tokens, filled with whole frames of clip slot_clip[s]. Every clip fills some slot, and the first and the last slot belong to the same clip. `clip_patches`: each clip has frames of 256 or of 1024 patches; both occur.
All inputs are finite; a program needn't handle non-finite values.
Results may differ from a plain program's by a relative error of at most 0.013.
The roundings to bfloat16 on the way count: a program that leaves them out, or rounds other values in their place, can miss the bound.
Values may be sent and summed in bfloat16 or wider, within the bound.
No kernel may reach another device: no remote copies, remote signals or barrier semaphores. Data moves between devices by JAX's collectives and lax.ppermute only.
A program may use at most 320 MiB of HBM per device.

v0:
```python
import jax
import jax.numpy as jnp
from jax import lax
from jax.sharding import PartitionSpec as P

HDIM = 72
PATCH_HI = 1024


epsilon = 1e-06
masked_score = -1000000000.0
highest = lax.Precision.HIGHEST


def normalize(row_block):
    centred = row_block - jnp.mean(row_block, axis=-1, keepdims=True)
    variance = jnp.mean(centred * centred, axis=-1, keepdims=True)
    inverse = lax.rsqrt(variance + epsilon)
    return (centred * inverse, inverse)


def norm_back(d_normed, normed, inverse):
    first_mean = jnp.mean(d_normed, axis=-1, keepdims=True)
    second_mean = jnp.mean(d_normed * normed, axis=-1, keepdims=True)
    return inverse * (d_normed - first_mean - normed * second_mean)


def gelu_tanh(values):
    return jax.nn.gelu(values, approximate=True)


def contract_rows(left, right):
    return lax.dot_general(
        left, right, (((0,), (0,)), ((), ())), preferred_element_type=jnp.float32
    )


def frame_scores(q_slots, k_slots, same_frame):
    scores = jnp.einsum(
        "sqhd,skhd->shqk", q_slots, k_slots, preferred_element_type=jnp.float32
    ) * HDIM ** (-0.5)
    return jnp.where(same_frame[:, None], scores, masked_score)


def shards(
    tokens,
    condition,
    q_weight,
    q_bias,
    k_weight,
    v_weight,
    v_bias,
    o_weight,
    o_bias,
    up_weight,
    up_bias,
    down_weight,
    down_bias,
    ada_weight,
    ada_bias,
    out_grad,
    slot_clip,
    clip_patches,
):
    own_rows = tokens.shape[0]
    model_width = tokens.shape[1]
    clip_count = condition.shape[0]
    local_width = q_weight.shape[1]
    slot_count = slot_clip.shape[0]
    group_rows = slot_count * PATCH_HI
    heads_here = local_width // HDIM
    narrow_index = lax.axis_index("narrow")
    slot_shape = (slot_count, PATCH_HI, heads_here, HDIM)
    score_scale = HDIM ** (-0.5)
    cond_float = condition.astype(jnp.float32)
    silu_cond = jax.nn.silu(cond_float).astype(jnp.bfloat16)
    mod_part = (
        jnp.einsum("cd,dke->cke", silu_cond, ada_weight, preferred_element_type=jnp.float32)
        + ada_bias
    )
    modulation = lax.all_gather(mod_part, "narrow", axis=2, tiled=True)
    row_index = narrow_index * own_rows + jnp.arange(own_rows, dtype=jnp.int32)
    row_clip = slot_clip[row_index // PATCH_HI]
    one_hot = (row_clip[:, None] == jnp.arange(clip_count, dtype=jnp.int32)[None, :]).astype(
        jnp.float32
    )
    row_mod = jnp.dot(
        one_hot, modulation.reshape(clip_count, 6 * model_width), precision=highest
    ).reshape(own_rows, 6, model_width)
    shift_one, scale_one, gate_one = (row_mod[:, 0], row_mod[:, 1], row_mod[:, 2])
    shift_two, scale_two, gate_two = (row_mod[:, 3], row_mod[:, 4], row_mod[:, 5])
    inputs = tokens.astype(jnp.float32)
    normed_one, inverse_one = normalize(inputs)
    attn_own = (normed_one * (1.0 + scale_one) + shift_one).astype(jnp.bfloat16)
    attn_in = lax.all_gather(attn_own, "narrow", axis=0, tiled=True)
    q_rows = (jnp.dot(attn_in, q_weight, preferred_element_type=jnp.float32) + q_bias).astype(
        jnp.bfloat16
    )
    k_rows = jnp.dot(attn_in, k_weight, preferred_element_type=jnp.float32).astype(jnp.bfloat16)
    v_rows = (jnp.dot(attn_in, v_weight, preferred_element_type=jnp.float32) + v_bias).astype(
        jnp.bfloat16
    )
    q_slots = q_rows.reshape(slot_shape)
    k_slots = k_rows.reshape(slot_shape)
    v_slots = v_rows.reshape(slot_shape)
    slot_patches = clip_patches[slot_clip]
    frame_id = jnp.arange(PATCH_HI, dtype=jnp.int32)[None, :] // slot_patches[:, None]
    same_frame = frame_id[:, :, None] == frame_id[:, None, :]
    scores = frame_scores(q_slots, k_slots, same_frame)
    row_max = jnp.max(scores, axis=-1, keepdims=True)
    exp_scores = jnp.exp(scores - row_max)
    totals = jnp.sum(exp_scores, axis=-1, keepdims=True)
    log_total = row_max + jnp.log(totals)
    attn_weights = (exp_scores / totals).astype(jnp.bfloat16)
    attended = jnp.einsum(
        "shqk,skhd->sqhd", attn_weights, v_slots, preferred_element_type=jnp.float32
    )
    attended = attended.reshape(group_rows, local_width).astype(jnp.bfloat16)
    row_part = attended
    attn_sum = lax.psum_scatter(
        jnp.dot(row_part, o_weight, preferred_element_type=jnp.float32),
        "narrow",
        scatter_dimension=0,
        tiled=True,
    )
    branch_one = attn_sum + o_bias
    middle = inputs + gate_one * branch_one
    normed_two, inverse_two = normalize(middle)
    mlp_own = (normed_two * (1.0 + scale_two) + shift_two).astype(jnp.bfloat16)
    mlp_in = lax.all_gather(mlp_own, "narrow", axis=0, tiled=True)
    pre_act = jnp.dot(mlp_in, up_weight, preferred_element_type=jnp.float32) + up_bias
    hidden = gelu_tanh(pre_act).astype(jnp.bfloat16)
    row_part = hidden
    down_sum = lax.psum_scatter(
        jnp.dot(row_part, down_weight, preferred_element_type=jnp.float32).astype(jnp.bfloat16),
        "narrow",
        scatter_dimension=0,
        tiled=True,
    ).astype(jnp.float32)
    branch_two = down_sum + down_bias
    block_out = (middle + gate_two * branch_two).astype(jnp.bfloat16)
    cotangent = out_grad.astype(jnp.float32)
    d_gate_two = cotangent * branch_two
    d_branch_two = (gate_two * cotangent).astype(jnp.bfloat16)
    d_branch_all = lax.all_gather(d_branch_two, "narrow", axis=0, tiled=True)
    d_hidden = jnp.dot(d_branch_all, down_weight.T, preferred_element_type=jnp.float32)
    grad_down_weight = contract_rows(hidden, d_branch_all)
    grad_down_bias = jnp.sum(d_branch_all, axis=0, dtype=jnp.float32)
    d_pre = jax.vjp(gelu_tanh, pre_act)[1](d_hidden)[0].astype(jnp.bfloat16)
    grad_up_weight = contract_rows(mlp_in, d_pre)
    grad_up_bias = jnp.sum(d_pre, axis=0, dtype=jnp.float32)
    row_part = d_pre
    d_mlp_in = lax.psum_scatter(
        jnp.dot(row_part, up_weight.T, preferred_element_type=jnp.float32),
        "narrow",
        scatter_dimension=0,
        tiled=True,
    )
    d_scale_two = d_mlp_in * normed_two
    d_middle = cotangent + norm_back(d_mlp_in * (1.0 + scale_two), normed_two, inverse_two)
    d_gate_one = d_middle * branch_one
    d_branch_one = (gate_one * d_middle).astype(jnp.bfloat16)
    d_attn_all = lax.all_gather(d_branch_one, "narrow", axis=0, tiled=True)
    grad_o_weight = contract_rows(attended, d_attn_all)
    grad_o_bias = jnp.sum(d_attn_all, axis=0, dtype=jnp.float32)
    d_attended = jnp.dot(d_attn_all, o_weight.T, preferred_element_type=jnp.float32).astype(
        jnp.bfloat16
    )
    d_attended = d_attended.reshape(slot_shape)
    recomputed = jnp.exp(frame_scores(q_slots, k_slots, same_frame) - log_total)
    d_weights = jnp.einsum(
        "sqhd,skhd->shqk", d_attended, v_slots, preferred_element_type=jnp.float32
    )
    d_scores = recomputed * (d_weights - jnp.sum(recomputed * d_weights, axis=-1, keepdims=True))
    d_scores = d_scores.astype(jnp.bfloat16)
    d_query = (
        (
            jnp.einsum("shqk,skhd->sqhd", d_scores, k_slots, preferred_element_type=jnp.float32)
            * score_scale
        )
        .astype(jnp.bfloat16)
        .reshape(group_rows, local_width)
    )
    d_key = (
        (
            jnp.einsum("shqk,sqhd->skhd", d_scores, q_slots, preferred_element_type=jnp.float32)
            * score_scale
        )
        .astype(jnp.bfloat16)
        .reshape(group_rows, local_width)
    )
    d_value = (
        jnp.einsum(
            "shqk,sqhd->skhd",
            recomputed.astype(jnp.bfloat16),
            d_attended,
            preferred_element_type=jnp.float32,
        )
        .astype(jnp.bfloat16)
        .reshape(group_rows, local_width)
    )
    grad_q_weight = contract_rows(attn_in, d_query)
    grad_q_bias = jnp.sum(d_query, axis=0, dtype=jnp.float32)
    grad_k_weight = contract_rows(attn_in, d_key)
    grad_v_weight = contract_rows(attn_in, d_value)
    grad_v_bias = jnp.sum(d_value, axis=0, dtype=jnp.float32)
    total = jnp.dot(d_query, q_weight.T, preferred_element_type=jnp.float32)
    total = total + jnp.dot(d_key, k_weight.T, preferred_element_type=jnp.float32)
    d_attn_in = lax.psum_scatter(
        total + jnp.dot(d_value, v_weight.T, preferred_element_type=jnp.float32),
        "narrow",
        scatter_dimension=0,
        tiled=True,
    )
    d_scale_one = d_attn_in * normed_one
    grad_tokens = d_middle + norm_back(d_attn_in * (1.0 + scale_one), normed_one, inverse_one)
    row_terms = jnp.stack(
        [d_attn_in, d_scale_one, d_gate_one, d_mlp_in, d_scale_two, d_gate_two], axis=1
    )
    d_mod_local = lax.dot_general(
        one_hot,
        row_terms.reshape(own_rows, 6 * model_width),
        (((0,), (0,)), ((), ())),
        precision=highest,
    ).reshape(clip_count, 6, model_width)
    d_mod_whole = lax.psum(d_mod_local, ("wide", "narrow"))
    d_modulation = lax.dynamic_slice_in_dim(d_mod_whole, narrow_index * local_width, local_width, 2)
    silu_float = silu_cond.astype(jnp.float32)
    grad_ada_weight = jnp.einsum("cd,cke->dke", silu_float, d_modulation, precision=highest)
    grad_ada_bias = jnp.sum(d_modulation, axis=0)
    d_silu_part = jnp.einsum(
        "cke,dke->cd", d_modulation, ada_weight.astype(jnp.float32), precision=highest
    )
    d_silu = lax.psum(d_silu_part, "narrow")
    grad_condition = jax.vjp(jax.nn.silu, cond_float)[1](d_silu)[0]
    (
        grad_q_weight,
        grad_q_bias,
        grad_k_weight,
        grad_v_weight,
        grad_v_bias,
        grad_o_weight,
        grad_o_bias,
        grad_up_weight,
        grad_up_bias,
        grad_down_weight,
        grad_down_bias,
    ) = lax.psum(
        (
            grad_q_weight,
            grad_q_bias,
            grad_k_weight,
            grad_v_weight,
            grad_v_bias,
            grad_o_weight,
            grad_o_bias,
            grad_up_weight,
            grad_up_bias,
            grad_down_weight,
            grad_down_bias,
        ),
        "wide",
    )
    return (
        block_out,
        grad_tokens,
        grad_condition,
        grad_q_weight,
        grad_q_bias,
        grad_k_weight,
        grad_v_weight,
        grad_v_bias,
        grad_o_weight,
        grad_o_bias,
        grad_up_weight,
        grad_up_bias,
        grad_down_weight,
        grad_down_bias,
        grad_ada_weight,
        grad_ada_bias,
    )


def solution(mesh):
    in_specs = (
        P(("wide", "narrow"), None),
        P(),
        P(None, "narrow"),
        P("narrow"),
        P(None, "narrow"),
        P(None, "narrow"),
        P("narrow"),
        P("narrow", None),
        P(),
        P(None, "narrow"),
        P("narrow"),
        P("narrow", None),
        P(),
        P(None, None, "narrow"),
        P(None, "narrow"),
        P(("wide", "narrow"), None),
        P("wide"),
        P(),
    )
    out_specs = (
        P(("wide", "narrow"), None),
        P(("wide", "narrow"), None),
        P(),
        P(None, "narrow"),
        P("narrow"),
        P(None, "narrow"),
        P(None, "narrow"),
        P("narrow"),
        P("narrow", None),
        P(),
        P(None, "narrow"),
        P("narrow"),
        P("narrow", None),
        P(),
        P(None, None, "narrow"),
        P(None, "narrow"),
    )
    return jax.shard_map(shards, mesh=mesh, in_specs=in_specs, out_specs=out_specs, check_vma=False)
```

profile of v0, /device:TPU:0, one launch (start us, length us, event | category | flops | bytes accessed | tf_op | source)
XLA Modules:
  0.0 1695.4 jit_solution(11846305217090919244)
XLA Ops:
  16.9 90.4 %all_gather.15 = f32[5,6,1152]{1,0,2:T(8,128)} all-gather(f32[5,6,288]{1,0,2:T(8,128)} %copy.81), channel_id=1, replica_groups=mesh['wide'=8,'narrow'=4] {'narrow'}, dimensions={2}, use_global_device_ids=true | all-gather | bytes 172800 | tf_op jit(solution)/shard_map/all_gather | solution.py:81
  112.1 5.7 fusion.72
  128.3 86.4 %all-gather.5.cloned.1.call-done = bf16[2048,1152]{1,0:T(8,128)(2,1)} async-done(((bf16[512,1152]{1,0:T(8,128)(2,1)}), bf16[2048,1152]{1,0:T(8,128)(2,1)}) %all-gather.5.cloned.1.call-update) | async-done | bytes 4718608 | tf_op jit(solution)/shard_map/all_gather | solution.py:95
  242.2 16.2 fusion.88
  258.4 13.4 fusion
  271.7 13.7 fusion.50
  294.0 159.2 %reduce-scatter.5.cloned.1.call-done = f32[512,1152]{1,0:T(8,128)} async-done(((f32[2048,1152]{1,0:T(8,128)}), f32[512,1152]{1,0:T(8,128)}) %reduce-scatter.5.cloned.1.call-update) | async-done | bytes 2359312 | tf_op jit(solution)/shard_map/reduce_scatter | solution.py:120
  464.2 89.7 %all-gather.9.cloned.1.call-done = bf16[2048,1152]{1,0:T(8,128)(2,1)} async-done(((bf16[512,1152]{1,0:T(8,128)(2,1)}), bf16[2048,1152]{1,0:T(8,128)(2,1)}) %all-gather.9.cloned.1.call-update) | async-done | bytes 4718608 | tf_op jit(solution)/shard_map/all_gather | solution.py:145
  554.0 12.1 fusion.92
  566.0 77.8 %all-gather.7.cloned.1.call-done = bf16[2048,1152]{1,0:T(8,128)(2,1)} async-done(((bf16[512,1152]{1,0:T(8,128)(2,1)}), bf16[2048,1152]{1,0:T(8,128)(2,1)}) %all-gather.7.cloned.1.call-update) | async-done | bytes 4718608 | tf_op jit(solution)/shard_map/all_gather | solution.py:130
  643.9 20.0 %convert_reduce_fusion.1 = (f32[1152]{0:T(1024)}, bf16[2048,1152]{1,0:T(8,128)(2,1)S(1)}, f32[2048,1152]{1,0:T(8,128)}) fusion(f32[2048,1152]{1,0:T(8,128)} %fusion.92, f32[1152]{0:T(1024)S(1)} %convert_element_type.141, bf16[2048,1152]{1,0:T(8,128)(2,1)} %all-gather.7.cloned.1.call-done, bf16[1152,1152]{1,0:T(8,128)(2,1)S(1)} %copy-done), kind=kOutput, calls=%fused_computation.26 | convolution fusion | flops 5490080768 | bytes 30974976 | tf_op jit(solution)/shard_map/dot_general | solution.py:131
  666.0 9.2 fusion.93
  677.0 12.3 convolution_convert_fusion
  690.0 145.2 %reduce-scatter.9.cloned.1.call-done = f32[512,1152]{1,0:T(8,128)} async-done(((f32[2048,1152]{1,0:T(8,128)}), f32[512,1152]{1,0:T(8,128)}) %reduce-scatter.9.cloned.1.call-update) | async-done | bytes 2359312 | tf_op jit(solution)/shard_map/reduce_scatter | solution.py:153
  838.3 85.7 %reduce-scatter.7.cloned.1.call-done = bf16[512,1152]{1,0:T(8,128)(2,1)} async-done(((bf16[2048,1152]{1,0:T(8,128)(2,1)}), bf16[512,1152]{1,0:T(8,128)(2,1)}) %reduce-scatter.7.cloned.1.call-update) | async-done | bytes 1179664 | tf_op jit(solution)/shard_map/reduce_scatter | solution.py:134
  924.0 6.5 multiply_convert_fusion.4
  930.6 90.0 %all-gather.11.cloned.1.call-done = bf16[2048,1152]{1,0:T(8,128)(2,1)} async-done(((bf16[512,1152]{1,0:T(8,128)(2,1)}), bf16[2048,1152]{1,0:T(8,128)(2,1)}) %all-gather.11.cloned.1.call-update) | async-done | bytes 4718608 | tf_op jit(solution)/shard_map/all_gather | solution.py:163
  1029.7 14.8 convert_reduce_fusion.4
  1044.5 22.7 %multiply_reduce_fusion = (f32[2,4,1024]{2,1,0:T(4,128)S(1)}, f32[2,4,1024,1024]{2,3,1,0:T(8,128)}) fusion(f32[2,4,1024,1024]{2,3,1,0:T(8,128)} %get-tuple-element.43, f32[2,4,1024]{2,1,0:T(4,128)S(1)} %bitcast.184, bf16[2,1024,4,72]{1,0,3,2:T(2,128)(2,1)} %reshape.329, bf16[2,1024,4,72]{1,0,3,2:T(2,128)(2,1)} %reshape.332), kind=kOutput, calls=%fused_computation.2 | convolution fusion | flops 1233117184 | bytes 69533696 | tf_op jit(solution)/shard_map/sqhd,skhd->shqk/dot_general | solution.py:171
  1067.3 28.4 %multiply_convert_fusion = bf16[2,4,1024,1024]{2,3,1,0:T(8,128)(2,1)} fusion(f32[2,4,1024,1024]{2,3,1,0:T(8,128)} %get-tuple-element.46, f32[2,4,1024,1024]{2,3,1,0:T(8,128)} %get-tuple-element.43, f32[2,4,1024]{2,1,0:T(4,128)S(1)} %get-tuple-element.45, f32[2,4,1024]{2,1,0:T(4,128)S(1)} %bitcast.185), kind=kLoop, calls=%fused_computation.1 | loop fusion | flops 33554432 | bytes 83951616 | tf_op jit(solution)/shard_map/convert_element_type | solution.py:175
  1095.7 12.4 fusion.49
  1108.1 9.4 convert_reduce_fusion.5
  1133.6 15.1 fusion.84
  1148.7 13.0 fusion.96
  1174.9 118.5 %reduce-scatter.11.cloned.1.call-done = f32[512,1152]{1,0:T(8,128)} async-done(((f32[2048,1152]{1,0:T(8,128)}), f32[512,1152]{1,0:T(8,128)}) %reduce-scatter.11.cloned.1.call-update) | async-done | bytes 2359312 | tf_op jit(solution)/shard_map/reduce_scatter | solution.py:209
  1308.3 15.1 copy.99
  1323.5 10.3 fusion.6
  1345.5 24.2 %all-reduce = (f32[288]{0:T(512)}, f32[288]{0:T(512)}, f32[1152]{0:T(1024)}, f32[1152]{0:T(1024)}, f32[1152]{0:T(1024)}) all-reduce(f32[288]{0:T(512)S(1)} %reduce_sum.159, f32[288]{0:T(512)S(1)} %reduce_sum.161, f32[1152]{0:T(1024)S(1)} %convert_reduce_fusion.2, ...), channel_id=1, replica_groups=mesh['wide'=8,'narrow'=4] {'wide'}, use_global_device_ids=true, to_apply=%region_19.20 | all-reduce | flops 4032 | bytes 32256 | tf_op jit(solution)/shard_map/psum | solution.py:248
  1377.5 80.2 %all-reduce.5.cloned.1.call-done = f32[5,6,1152]{2,0,1:T(8,128)} async-done(((f32[5,6,1152]{2,0,1:T(8,128)}), f32[5,6,1152]{2,0,1:T(8,128)}) %all-reduce.5.cloned.1.call-update) | async-done | bytes 138256 | tf_op jit(solution)/shard_map/psum | solution.py:226
  1463.3 20.3 %psum.92 = f32[5,1152]{1,0:T(8,128)S(1)} all-reduce(f32[5,1152]{1,0:T(8,128)S(1)} %convolution_bitcast_fusion), channel_id=1, replica_groups=mesh['wide'=8,'narrow'=4] {'narrow'}, use_global_device_ids=true, to_apply=%region_16.17 | all-reduce | flops 5760 | bytes 46080 | tf_op jit(solution)/shard_map/psum | solution.py:234
  1483.6 7.6 fusion.60
  1491.9 183.0 %all-reduce.7.cloned.1.call-done = (f32[1152,288]{0,1:T(8,128)}, f32[1152,288]{0,1:T(8,128)}, f32[1152,288]{0,1:T(8,128)}, f32[288,1152]{1,0:T(8,128)}, f32[1152,1152]{1,0:T(8,128)}, /*index=5*/f32[1152,1152]{1,0:T(8,128)}) async-done(((f32[1152,288]{0,1:T(8,128)}, f32[1152,288]{0,1:T(8,128)}, f32[1152,288]{0,1:T(8,128)}, f32[288,1152]{1,0:T(8,128)}, f32[1152,1152]{1,0:T(8,128)}, ...) | async-done | bytes 15925264 | tf_op jit(solution)/shard_map/psum | solution.py:248
  (226 shorter events, 171.7 us)
Async XLA Ops:
  7.2 636.7 %copy-start = (bf16[1152,1152]{1,0:T(8,128)(2,1)S(1)}, bf16[1152,1152]{1,0:T(8,128)(2,1)}, u32[]{:S(2)}) copy-start(bf16[1152,1152]{1,0:T(8,128)(2,1)} %param.27) | copy-start | bytes 7962628
  7.2 207.5 %all-gather.5.cloned.1.call-start = ((), (), s32[]{:S(2)}) async-start(), calls=%async_computation.4 | async-start | bytes 5898240 | tf_op jit(solution)/shard_map/all_gather | solution.py:95
  10.2 107.7 %copy-start.41 = (f32[512]{0:T(512)}, f32[512]{0:T(512)S(1)}, u32[]{:S(2)}) copy-start(f32[512]{0:T(512)S(1)} %broadcast_multiply_fusion.5) | copy-start | bytes 6148
  11.9 106.0 %copy-start.45 = (f32[512]{0:T(512)}, f32[512]{0:T(512)S(1)}, u32[]{:S(2)}) copy-start(f32[512]{0:T(512)S(1)} %add_rsqrt_fusion.1) | copy-start | bytes 6148
  112.1 10.8 copy-start.6
  124.6 90.1 %copy-start.34 = (bf16[1152,288]{0,1:T(8,128)(2,1)S(1)}, bf16[1152,288]{0,1:T(8,128)(2,1)}, u32[]{:S(2)}) copy-start(bf16[1152,288]{0,1:T(8,128)(2,1)} %param.20) | copy-start | bytes 1990660
  124.6 328.6 %reduce-scatter.5.cloned.1.call-start = ((), (), s32[]{:S(2)}) async-start(), calls=%async_computation.5 | async-start | bytes 11796480 | tf_op jit(solution)/shard_map/reduce_scatter | solution.py:120
  258.3 13.4 copy-start.28
  293.3 260.7 %all-gather.9.cloned.1.call-start = ((), (), s32[]{:S(2)}) async-start(), calls=%async_computation.8 | async-start | bytes 5898240 | tf_op jit(solution)/shard_map/all_gather | solution.py:145
  294.0 162.4 %copy-start.43 = (f32[1152]{0:T(1024)}, f32[1152]{0:T(1024)S(1)}, u32[]{:S(2)}) copy-start(f32[1152]{0:T(1024)S(1)} %convert_element_type.139) | copy-start | bytes 13828
  456.4 7.2 copy-start.4
  463.6 180.3 %all-gather.7.cloned.1.call-start = ((), (), s32[]{:S(2)}) async-start(), calls=%async_computation.6 | async-start | bytes 5898240 | tf_op jit(solution)/shard_map/all_gather | solution.py:130
  464.1 371.0 %reduce-scatter.9.cloned.1.call-start = ((), (), s32[]{:S(2)}) async-start(), calls=%async_computation.9 | async-start | bytes 11796480 | tf_op jit(solution)/shard_map/reduce_scatter | solution.py:153
  675.3 248.7 %reduce-scatter.7.cloned.1.call-start = ((), (), s32[]{:S(2)}) async-start(), calls=%async_computation.7 | async-start | bytes 5898240 | tf_op jit(solution)/shard_map/reduce_scatter | solution.py:134
  689.3 145.9 %copy-start.5 = (f32[512,1152]{1,0:T(8,128)S(1)}, f32[512,1152]{1,0:T(8,128)}, u32[]{:S(2)}) copy-start(f32[512,1152]{1,0:T(8,128)} %copy-done.4) | copy-start | bytes 7077892
  689.3 331.4 %all-gather.11.cloned.1.call-start = ((), (), s32[]{:S(2)}) async-start(), calls=%async_computation.10 | async-start | bytes 5898240 | tf_op jit(solution)/shard_map/all_gather | solution.py:163
  930.6 362.8 %reduce-scatter.11.cloned.1.call-start = ((), (), s32[]{:S(2)}) async-start(), calls=%async_computation.11 | async-start | bytes 11796480 | tf_op jit(solution)/shard_map/reduce_scatter | solution.py:209
  1108.1 9.4 copy-start.29
  1119.0 9.1 copy-start.19
  1133.5 324.2 %all-reduce.5.cloned.1.call-start = ((), (), s32[]{:S(2)}) async-start(), calls=%async_computation.12 | async-start | bytes 442368 | tf_op jit(solution)/shard_map/psum | solution.py:226
  1148.7 13.0 copy-start.22
  1161.7 5.2 copy-start.20
  1161.7 10.5 slice-start.2
  1166.9 5.2 copy-start.24
  1166.9 5.2 slice-start.3
  1174.9 121.9 %copy-start.42 = (f32[512]{0:T(512)S(1)}, f32[512]{0:T(512)}, u32[]{:S(2)}) copy-start(f32[512]{0:T(512)} %copy-done.41) | copy-start | bytes 6148
  1174.9 121.9 %copy-start.46 = (f32[512]{0:T(512)S(1)}, f32[512]{0:T(512)}, u32[]{:S(2)}) copy-start(f32[512]{0:T(512)} %copy-done.45) | copy-start | bytes 6148
  1308.3 15.2 copy-start.48
  1323.5 10.5 copy-start.18
  1333.8 341.1 %all-reduce.7.cloned.1.call-start = ((), (), s32[]{:S(2)}) async-start(), calls=%async_computation.13 | async-start | bytes 31850496 | tf_op jit(solution)/shard_map/psum | solution.py:248
  1342.4 27.3 %copy-start.8 = (bf16[512,1152]{1,0:T(8,128)(2,1)S(1)}, bf16[512,1152]{1,0:T(8,128)(2,1)}, u32[]{:S(2)}) copy-start(bf16[512,1152]{1,0:T(8,128)(2,1)} %param.18) | copy-start | bytes 3538948
  1377.5 106.0 %copy-start.40 = (bf16[5,1152]{1,0:T(8,128)(2,1)S(1)}, bf16[5,1152]{1,0:T(8,128)(2,1)}, u32[]{:S(2)}) copy-start(bf16[5,1152]{1,0:T(8,128)(2,1)} %param.19) | copy-start | bytes 34564
  (41 other events, 110.4 us)
Sparse Core Ops, SparseCore 0:
  124.7 89.9 all-gather.4
  293.4 159.7 reduce-scatter.4
  463.7 90.2 all-gather.8
  556.0 87.8 all-gather.6
  675.4 159.7 reduce-scatter.8
  837.9 86.0 reduce-scatter.6
  930.7 89.9 all-gather.10
  1133.6 159.7 reduce-scatter.10
  1333.9 123.8 all-reduce.4
  1463.6 211.2 all-reduce.6
where the time goes:
time: 1700 us
  waiting for transfers between devices  1120 us (66%)
  matrix products  257 us (15%)
  blocking collectives  135 us (8%)
  other arithmetic  92 us (5%)
  local copies, waits for them, and re-layouts  79.4 us (5%)
    psum x1, waiting for transfers between devices, shards(): lax.psum((grad_q_weight, grad_q_bias, grad_k_weight, grad_v_weight, grad_...  183 us
    reduce_scatter x1, waiting for transfers between devices, shards(): lax.psum_scatter(jnp.dot(row_part, o_weight, preferred_element_type=jnp.f...  159 us
    reduce_scatter x1, waiting for transfers between devices, shards(): lax.psum_scatter(jnp.dot(row_part, up_weight.T, preferred_element_type=jn...  145 us
    reduce_scatter x1, waiting for transfers between devices, shards(): lax.psum_scatter(total + jnp.dot(d_value, v_weight.T, preferred_element_t...  118 us
    all_gather x1, blocking collectives, shards(): modulation = lax.all_gather(mod_part, 'narrow', axis=2, tiled=True)  90.4 us
    all_gather x1, waiting for transfers between devices, shards(): d_attn_all = lax.all_gather(d_branch_one, 'narrow', axis=0, tiled=True)  90 us
    all_gather x1, waiting for transfers between devices, shards(): d_branch_all = lax.all_gather(d_branch_two, 'narrow', axis=0, tiled=True)  89.7 us
    all_gather x1, waiting for transfers between devices, shards(): attn_in = lax.all_gather(attn_own, 'narrow', axis=0, tiled=True)  86.4 us
  transfers between devices with their start and end apart: 10, of which 10 were waited for; matrix products, arithmetic and copies ran while one was open for 6% of the time, Pallas kernels for 0%

commit v1 on v0

v1 whole, which is shorter than its diff:
```python
import functools

import jax
import jax.numpy as jnp
from jax import lax
from jax.experimental import pallas as pl
from jax.experimental.pallas import tpu as pltpu
from jax.sharding import PartitionSpec as P

HDIM = 72
PATCH_HI = 1024
BLOCK = 256
ROW_BLOCK = 256
HIDDEN_BLOCK = 384
VMEM_LIMIT = 48 * 1024 * 1024

epsilon = 1e-06
highest = lax.Precision.HIGHEST
EXP2_SCALE = HDIM ** (-0.5) * 1.4426950408889634
f32 = jnp.float32
bf16 = jnp.bfloat16


def normalize(row_block):
    centred = row_block - jnp.mean(row_block, axis=-1, keepdims=True)
    variance = jnp.mean(centred * centred, axis=-1, keepdims=True)
    inverse = lax.rsqrt(variance + epsilon)
    return (centred * inverse, inverse)


def norm_back(d_normed, normed, inverse):
    first_mean = jnp.mean(d_normed, axis=-1, keepdims=True)
    second_mean = jnp.mean(d_normed * normed, axis=-1, keepdims=True)
    return inverse * (d_normed - first_mean - normed * second_mean)


def gelu_and_slope(values):
    root = (2.0 / jnp.pi) ** 0.5
    square = values * values
    tanh = jnp.tanh(root * (values + 0.044715 * (square * values)))
    half = 0.5 * (1.0 + tanh)
    slope = half + 0.5 * values * (1.0 - tanh * tanh) * (root + (3 * 0.044715 * root) * square)
    return values * half, slope


def dot(left, right):
    return jnp.dot(left, right, preferred_element_type=f32)


def dot_t(left, right):
    return lax.dot_general(left, right, (((1,), (1,)), ((), ())), preferred_element_type=f32)


def contract_rows(left, right):
    return lax.dot_general(left, right, (((0,), (0,)), ((), ())), preferred_element_type=f32)


def left_t_right_t(left, right):
    return lax.dot_general(left, right, (((0,), (1,)), ((), ())), preferred_element_type=f32)


def kernel_call(kernel, outs, **options):
    return pl.pallas_call(
        kernel,
        out_shape=outs,
        compiler_params=pltpu.CompilerParams(vmem_limit_bytes=VMEM_LIMIT),
        cost_estimate=pl.CostEstimate(flops=0, bytes_accessed=1024, transcendentals=0),
        **options,
    )


def whole(array):
    return pl.BlockSpec(array.shape, lambda *_: (0,) * len(array.shape))


def row_call(body, rows_in, vectors, out_types, term_count=0):
    rows, width = rows_in[0].shape[0], vectors[0].shape[1]
    step_rows = min(ROW_BLOCK, rows)
    rows_in = [each if isinstance(each, tuple) else (each, 0) for each in rows_in]

    def kernel(*refs):
        row_refs = refs[: len(rows_in)]
        vector_refs = refs[len(rows_in) : len(rows_in) + len(vectors)]
        out_refs = refs[len(rows_in) + len(vectors) :]
        outs, terms = body([ref[...] for ref in row_refs], vector_refs)
        for ref, out in zip(out_refs, outs):
            ref[...] = out.astype(ref.dtype)
        if term_count:
            sums_ref = refs[-1]

            @pl.when(pl.program_id(0) == 0)
            def _():
                sums_ref[...] = jnp.zeros_like(sums_ref)

            for index, term in enumerate(terms):
                sums_ref[index : index + 1, :] += jnp.sum(term, axis=0, keepdims=True)

    outs = [jax.ShapeDtypeStruct((rows, width), kind) for kind in out_types]
    out_specs = [pl.BlockSpec((step_rows, width), lambda index: (index, 0))] * len(outs)
    if term_count:
        outs.append(jax.ShapeDtypeStruct((8, width), f32))
        out_specs.append(pl.BlockSpec((8, width), lambda index: (0, 0)))
    return kernel_call(
        kernel,
        outs,
        grid=(rows // step_rows,),
        in_specs=[
            pl.BlockSpec((step_rows, each.shape[1]), lambda index, first=first: (first // step_rows + index, 0))
            for each, first in rows_in
        ]
        + [whole(each) for each in vectors],
        out_specs=out_specs,
    )(*(each for each, _ in rows_in), *vectors)


def modulated_rows_kernel(row_count, *refs):
    mod_ref, out_ref = refs[-2:]
    for index, ref in enumerate(refs[:row_count]):
        normed = normalize(ref[...].astype(f32))[0]
        out_ref[index] = (normed * (1.0 + mod_ref[1:2, :]) + mod_ref[0:1, :]).astype(bf16)


def modulated_rows(row_blocks, modulation):
    rows, width = row_blocks[0].shape
    count = len(row_blocks)
    out = kernel_call(
        functools.partial(modulated_rows_kernel, count),
        jax.ShapeDtypeStruct((count, rows, width), bf16),
        grid=(rows // ROW_BLOCK,),
        in_specs=[pl.BlockSpec((ROW_BLOCK, width), lambda index: (index, 0))] * count
        + [whole(modulation)],
        out_specs=pl.BlockSpec((count, ROW_BLOCK, width), lambda index: (0, index, 0)),
    )(*row_blocks, modulation)
    return out.reshape(count * rows, width)


def qkv_kernel(rows_ref, pack_ref, bias_ref, out_ref):
    columns = out_ref.shape[1]
    rows = dot_t(rows_ref[...], pack_ref[:columns]) + bias_ref[...].astype(f32)
    out_ref[...] = rows.astype(bf16)


def qkv_rows(rows, pack, bias):
    columns = pack.shape[0] // 4 * 3
    bias = bias.reshape(1, columns)
    return kernel_call(
        qkv_kernel,
        jax.ShapeDtypeStruct((rows.shape[0], columns), bf16),
        grid=(rows.shape[0] // BLOCK,),
        in_specs=[
            pl.BlockSpec((BLOCK, rows.shape[1]), lambda index: (index, 0)),
            whole(pack),
            whole(bias),
        ],
        out_specs=pl.BlockSpec((BLOCK, columns), lambda index: (index, 0)),
    )(rows, pack, bias)


def frame_loop(patches_ref, rows, heads, stages):
    is_full = patches_ref[0] == PATCH_HI
    first, second, third = stages

    def run(full):
        units = [(block * BLOCK, head) for block in range(rows // BLOCK) for head in range(heads)]
        begun = first(*units[0], full)
        done = None
        for at, unit in enumerate(units):
            coming = first(*units[at + 1], full) if at + 1 < len(units) else None
            if done is not None:
                third(*units[at - 1], full, done)
            done = second(*unit, full, begun)
            begun = coming
        third(*units[-1], full, done)

    @pl.when(is_full)
    def _():
        run(True)

    @pl.when(jnp.logical_not(is_full))
    def _():
        run(False)


def attention_forward_kernel(
    first_row, patches_ref, qkv_ref, attended_ref, turned_ref, lse_ref, out_scratch
):
    heads = qkv_ref.shape[1] // (3 * HDIM)

    def columns(start, full, part, head):
        at = (part * heads + head) * HDIM
        rows = slice(0, PATCH_HI) if full else slice(first_row + start, first_row + start + BLOCK)
        return qkv_ref[rows, at : at + HDIM]

    def scores(start, head, full):
        return dot_t(columns(start, full, 1, head), columns(start, False, 0, head))

    def softmax(start, head, full, logits):
        out_rows = slice(start, start + BLOCK)
        top = jnp.max(logits, axis=0, keepdims=True) * EXP2_SCALE
        exp_scores = jnp.exp2(logits * EXP2_SCALE - top)
        total = jnp.sum(exp_scores, axis=0, keepdims=True)
        lse_ref[head : head + 1, out_rows] = top + jnp.log2(total)
        return (exp_scores * (1.0 / total)).astype(bf16)

    def values(start, head, full, weights):
        out_scratch[head * HDIM : (head + 1) * HDIM, start : start + BLOCK] = contract_rows(
            columns(start, full, 2, head), weights
        )

    frame_loop(patches_ref, lse_ref.shape[1], heads, (scores, softmax, values))
    attended_ref[...] = out_scratch[...].T.astype(bf16)
    turned_ref[...] = out_scratch[...].astype(bf16)


VMEM_SPEC = pl.BlockSpec(memory_space=pltpu.VMEM)
SMEM_SPEC = pl.BlockSpec(memory_space=pltpu.SMEM)


def attention_forward(qkv, patches, first_row, rows):
    width = qkv.shape[1] // 3
    return kernel_call(
        functools.partial(attention_forward_kernel, first_row),
        (
            jax.ShapeDtypeStruct((rows, width), bf16),
            jax.ShapeDtypeStruct((width, rows), bf16),
            jax.ShapeDtypeStruct((width // HDIM, rows), f32),
        ),
        in_specs=[SMEM_SPEC, VMEM_SPEC],
        out_specs=(VMEM_SPEC, VMEM_SPEC, VMEM_SPEC),
        scratch_shapes=[pltpu.VMEM((width, rows), f32)],
    )(patches, qkv)


def attention_backward_kernel(first_row, first, last, *refs):
    patches_ref, qkv_ref, d_rows_ref, pack_ref, lse_ref = refs[:5]
    sums_ref = refs[5] if not first else None
    d_query_ref, d_query_turned_ref, d_kv_ref, *rest = refs[5 if first else 6 :]
    d_kv_turned_ref = rest[0] if last else None
    query_scratch, kv_scratch, d_scratch = rest[-3:]
    local = d_query_ref.shape[1]
    heads = local // HDIM
    scale = HDIM ** (-0.5)
    kv_scratch[...] = jnp.zeros_like(kv_scratch) if first else sums_ref[...]
    d_scratch[...] = dot_t(d_rows_ref[...], pack_ref[3 * local :]).astype(bf16)

    def columns(start, full, part, head):
        at = (part * heads + head) * HDIM
        rows = slice(0, PATCH_HI) if full else slice(first_row + start, first_row + start + BLOCK)
        return qkv_ref[rows, at : at + HDIM]

    def d_out(start, head):
        return d_scratch[start : start + BLOCK, head * HDIM : (head + 1) * HDIM]

    def products(start, head, full):
        logits = dot_t(columns(start, full, 1, head), columns(start, False, 0, head))
        return logits, dot_t(columns(start, full, 2, head), d_out(start, head))

    def d_softmax(start, head, full, pair):
        logits, d_weights = pair
        probs = jnp.exp2(logits * EXP2_SCALE - lse_ref[head : head + 1, start : start + BLOCK])
        delta = jnp.sum(probs * d_weights, axis=0, keepdims=True)
        return probs.astype(bf16), (probs * (d_weights - delta)).astype(bf16)

    def gradients(start, head, full, pair):
        probs, d_scores = pair
        at = slice(head * HDIM, (head + 1) * HDIM)
        v_at = slice(local + head * HDIM, local + (head + 1) * HDIM)
        k_rows = slice(0, PATCH_HI) if full else slice(first_row + start, first_row + start + BLOCK)
        query_scratch[at, start : start + BLOCK] = (
            contract_rows(columns(start, full, 1, head), d_scores) * scale
        )
        kv_scratch[at, k_rows] += left_t_right_t(columns(start, False, 0, head), d_scores) * scale
        kv_scratch[v_at, k_rows] += left_t_right_t(d_out(start, head), probs)

    frame_loop(patches_ref, lse_ref.shape[1], heads, (products, d_softmax, gradients))
    d_query_ref[...] = query_scratch[...].T.astype(bf16)
    d_query_turned_ref[...] = query_scratch[...].astype(bf16)
    if last:
        d_kv_ref[...] = kv_scratch[...].T.astype(bf16)
        d_kv_turned_ref[...] = kv_scratch[...].astype(bf16)
    else:
        d_kv_ref[...] = kv_scratch[...]


def attention_backward(qkv, d_rows, pack, lse, patches, sums, first_row, last):
    local = pack.shape[0] // 4
    rows = d_rows.shape[0]
    first = sums is None
    turned = (2 * local, PATCH_HI)
    extra = [] if first else [sums]
    outs = [jax.ShapeDtypeStruct((rows, local), bf16), jax.ShapeDtypeStruct((local, rows), bf16)]
    if last:
        outs += [jax.ShapeDtypeStruct(turned[::-1], bf16), jax.ShapeDtypeStruct(turned, bf16)]
    else:
        outs.append(jax.ShapeDtypeStruct(turned, f32))
    return kernel_call(
        functools.partial(attention_backward_kernel, first_row, first, last),
        outs,
        in_specs=[SMEM_SPEC] + [VMEM_SPEC] * (4 + len(extra)),
        out_specs=[VMEM_SPEC] * len(outs),
        scratch_shapes=[
            pltpu.VMEM((local, rows), f32),
            pltpu.VMEM(turned, f32),
            pltpu.VMEM((rows, local), bf16),
        ],
    )(patches, qkv, d_rows, pack, lse, *extra)


def feed_forward_kernel(last_types, shard_count, *refs):
    x_ref, grad_ref, mod_ref, bias_ref = refs[:4]
    up_refs = refs[4 : 4 + shard_count]
    down_refs = refs[4 + shard_count : 4 + 2 * shard_count]
    hidden_ref, d_pre_ref, d_branch_ref, d_mlp_ref, branch_ref, sums_ref = refs[-8:-2]
    d_mlp_scratch, branch_scratch = refs[-2:]

    @pl.when(pl.program_id(0) == 0)
    def _():
        d_mlp_scratch[...] = jnp.zeros_like(d_mlp_scratch)
        branch_scratch[...] = jnp.zeros_like(branch_scratch)
        d_branch_ref[...] = (mod_ref[5:6, :] * grad_ref[...].astype(f32)).astype(bf16)

    sums_ref[...] = jnp.zeros_like(sums_ref)
    rows = x_ref.shape[0]
    for start in range(0, rows, BLOCK):
        block = slice(start, start + BLOCK)
        d_mlp, branch = 0.0, 0.0
        for shard in range(shard_count):
            pre_act = dot(x_ref[block], up_refs[shard][...]) + bias_ref[shard].astype(f32)
            hidden, slope = gelu_and_slope(pre_act)
            d_pre = (dot_t(d_branch_ref[block], down_refs[shard][...]) * slope).astype(bf16)
            hidden = hidden.astype(bf16)
            hidden_ref[shard, block] = hidden
            d_pre_ref[shard, block] = d_pre
            sums_ref[shard : shard + 1] += jnp.sum(d_pre.astype(f32), axis=0, keepdims=True)
            d_mlp = d_mlp + dot_t(d_pre, up_refs[shard][...])
            branch = branch + dot(hidden, down_refs[shard][...])
        d_mlp_scratch[block] += d_mlp
        branch_scratch[block] += branch

    @pl.when(pl.program_id(0) == pl.num_programs(0) - 1)
    def _():
        d_mlp_ref[...] = d_mlp_scratch[...].astype(d_mlp_ref.dtype)
        branch_ref[...] = branch_scratch[...].astype(branch_ref.dtype)


def feed_forward(rows, grad, modulation, biases, ups, downs, sum_type):
    row_count, width = rows.shape
    shard_count = len(ups)
    hidden_local = biases.shape[-1]
    step = HIDDEN_BLOCK if hidden_local % HIDDEN_BLOCK == 0 else hidden_local
    in_specs = [whole(rows), whole(grad), whole(modulation)]
    in_specs.append(pl.BlockSpec((shard_count, 1, step), lambda index: (0, 0, index)))
    for _, first in ups:
        in_specs.append(pl.BlockSpec((width, step), lambda index, first=first: (0, first + index)))
    for _, first in downs:
        in_specs.append(pl.BlockSpec((step, width), lambda index, first=first: (index, first)))
    by_shard = pl.BlockSpec((shard_count, row_count, step), lambda index: (0, 0, index))
    flat = jax.ShapeDtypeStruct((row_count, width), sum_type)
    return kernel_call(
        functools.partial(feed_forward_kernel, sum_type, shard_count),
        [
            jax.ShapeDtypeStruct((shard_count, row_count, hidden_local), bf16),
            jax.ShapeDtypeStruct((shard_count, row_count, hidden_local), bf16),
            jax.ShapeDtypeStruct((row_count, width), bf16),
            flat,
            flat,
            jax.ShapeDtypeStruct((8, hidden_local), f32),
        ],
        grid=(hidden_local // step,),
        in_specs=in_specs,
        out_specs=[by_shard, by_shard]
        + [pl.BlockSpec((row_count, width), lambda index: (0, 0))] * 3
        + [pl.BlockSpec((8, step), lambda index: (0, index))],
        scratch_shapes=[pltpu.VMEM((row_count, width), f32)] * 2,
    )(rows, grad, modulation, biases, *(each for each, _ in ups), *(each for each, _ in downs))


def mlp_gradient_kernel(member_count, *refs):
    out_ref = refs[-1]
    is_up = pl.program_id(0) % 2 == 0
    pieces, _, rows, width = out_ref.shape

    def store(lefts, rights):
        total = sum(contract_rows(left, right) for left, right in zip(lefts, rights))
        out_ref[:, 0] = total.astype(bf16).reshape(pieces, rows, width)

    groups = [refs[at * member_count : (at + 1) * member_count] for at in range(4)]
    x_refs, d_branch_refs, hidden_refs, d_pre_refs = groups

    @pl.when(is_up)
    def _():
        store([ref[...] for ref in x_refs], [ref[0] for ref in d_pre_refs])

    @pl.when(jnp.logical_not(is_up))
    def _():
        store([ref[0] for ref in hidden_refs], [ref[...] for ref in d_branch_refs])


def mlp_gradients(x_rows, d_branch_rows, hidden, d_pre, pieces):
    shard_count, row_count, hidden_local = hidden[0].shape
    width = x_rows[0].shape[1]
    rows = hidden_local // pieces
    if hidden_local != width or rows % 16:
        parts = []
        for shard in range(shard_count):
            up = sum(contract_rows(left, right[shard]) for left, right in zip(x_rows, d_pre))
            down = sum(contract_rows(left[shard], right) for left, right in zip(hidden, d_branch_rows))
            parts += [up.reshape(pieces, rows, width), down.reshape(pieces, rows, width)]
        return jnp.stack(parts, axis=1).astype(bf16)
    by_shard = pl.BlockSpec((1, row_count, hidden_local), lambda index: (index // 2, 0, 0))
    return kernel_call(
        functools.partial(mlp_gradient_kernel, len(x_rows)),
        jax.ShapeDtypeStruct((pieces, 2 * shard_count, rows, width), bf16),
        grid=(2 * shard_count,),
        in_specs=[whole(each) for each in (*x_rows, *d_branch_rows)]
        + [by_shard] * (2 * len(x_rows)),
        out_specs=pl.BlockSpec((pieces, 1, rows, width), lambda index: (0, index, 0, 0)),
    )(*x_rows, *d_branch_rows, *hidden, *d_pre)


def attn_gradient_kernel(member_count, *refs):
    core_ref, in_ref, d_kv_ref = refs[:3]
    d_query_refs, d_branch_refs = refs[3 : 3 + member_count], refs[3 + member_count : 3 + 2 * member_count]
    attended_refs = refs[3 + 2 * member_count : -4]
    keep_ref, send_ref, sums_ref, out_ref = refs[-4:]
    local, rows = d_query_refs[0].shape
    query = sum(
        dot(ref[...], in_ref[at * rows : (at + 1) * rows]) for at, ref in enumerate(d_query_refs)
    )
    out_ref[:local] = query.astype(bf16)
    out_ref[local : 3 * local] = dot(d_kv_ref[...], in_ref[...]).astype(bf16)
    start, out = 0, 0.0
    for ref in attended_refs:
        first = start % rows
        out = out + dot(ref[...], d_branch_refs[start // rows][first : first + ref.shape[1]])
        start += ref.shape[1]
    out_ref[3 * local :] = out.astype(bf16)
    sums_ref[:local] = sum(
        jnp.sum(ref[...].astype(f32), axis=1, keepdims=True) for ref in d_query_refs
    )
    sums_ref[local:] = jnp.sum(d_kv_ref[...].astype(f32), axis=1, keepdims=True)
    if len(keep_ref.shape) == 2:
        keep_ref[...] = out_ref[...]
    else:
        core = core_ref[0]
        chips, piece_rows, _ = keep_ref.shape
        for chip in range(chips):
            kept = pl.multiple_of((2 * chip + core) * piece_rows, 16)
            sent = pl.multiple_of((2 * chip + 1 - core) * piece_rows, 16)
            keep_ref[chip] = out_ref[pl.ds(kept, piece_rows)]
            send_ref[chip] = out_ref[pl.ds(sent, piece_rows)]


def attn_gradients(attn_in, d_kv, d_query, d_branch_rows, attended, core, chips):
    width = attn_in.shape[1]
    local = d_query[0].shape[0]
    rows = 4 * local // (2 * chips)
    part = jax.ShapeDtypeStruct((chips, rows, width), bf16)
    if rows % 16:
        parts = (jax.ShapeDtypeStruct((4 * local, width), bf16), jax.ShapeDtypeStruct((8, 128), bf16))
    else:
        parts = (part, part)
    keep, send, sums = kernel_call(
        functools.partial(attn_gradient_kernel, len(d_query)),
        (*parts, jax.ShapeDtypeStruct((3 * local, 1), f32)),
        in_specs=[SMEM_SPEC] + [VMEM_SPEC] * (2 + 2 * len(d_query) + len(attended)),
        out_specs=(VMEM_SPEC, VMEM_SPEC, VMEM_SPEC),
        scratch_shapes=[pltpu.VMEM((4 * local, width), bf16)],
    )(core.reshape(1), attn_in, d_kv, *d_query, *d_branch_rows, *attended)
    if rows % 16:
        both = keep.reshape(chips, 2, rows, width)
        keep = lax.dynamic_index_in_dim(both, core, 1, keepdims=False)
        send = lax.dynamic_index_in_dim(both, 1 - core, 1, keepdims=False)
    return (keep, send), sums


def attn_outputs_kernel(core_ref, own_ref, other_ref, *out_refs):
    core = core_ref[0]
    rows = own_ref.shape[1]
    for at, ref in enumerate(out_refs):
        ref[pl.ds(pl.multiple_of(core * rows, 16), rows)] = own_ref[at].astype(f32)
        ref[pl.ds(pl.multiple_of((1 - core) * rows, 16), rows)] = other_ref[at].astype(f32)


def attn_outputs(own, other, core):
    chips, rows, width = own.shape
    if chips != 4 or rows % 16:
        both = jnp.where(core == 0, jnp.stack([own, other], 1), jnp.stack([other, own], 1))
        q, k, v, o = jnp.split(both.astype(f32).reshape(-1, width), 4)
    else:
        part = jax.ShapeDtypeStruct((2 * rows, width), f32)
        q, k, v, o = kernel_call(
            attn_outputs_kernel,
            [part] * 4,
            in_specs=[SMEM_SPEC, VMEM_SPEC, VMEM_SPEC],
            out_specs=[VMEM_SPEC] * 4,
        )(core.reshape(1), own, other)
    return q.T, k.T, v.T, o


def split_pieces_kernel(chip_ref, keep_ref, flipped_ref, own_ref, *send_refs):
    for mask, ref in enumerate((own_ref, *send_refs)):
        chip = chip_ref[0] ^ mask
        ref[...] = (keep_ref[chip].astype(f32) + flipped_ref[chip].astype(f32)).astype(bf16)


def split_pieces(keep, flipped, chip):
    piece = jax.ShapeDtypeStruct(keep.shape[1:], bf16)
    return kernel_call(
        split_pieces_kernel,
        [piece] * keep.shape[0],
        in_specs=[SMEM_SPEC, VMEM_SPEC, VMEM_SPEC],
        out_specs=[VMEM_SPEC] * keep.shape[0],
    )(chip.reshape(1), keep, flipped)


def add_kernel(*refs):
    total = sum([ref[...].astype(f32) for ref in refs[1:-1]], refs[0][...].astype(f32))
    refs[-1][...] = total.astype(bf16)


def add_arrays(*arrays):
    return kernel_call(
        add_kernel,
        jax.ShapeDtypeStruct(arrays[0].shape, bf16),
        in_specs=[VMEM_SPEC] * len(arrays),
        out_specs=VMEM_SPEC,
    )(*arrays)


def cut_kernel(in_ref, *out_refs):
    for at, ref in enumerate(out_refs):
        ref[...] = in_ref[at]


def cut(array):
    part = jax.ShapeDtypeStruct(array.shape[1:], array.dtype)
    return kernel_call(
        cut_kernel, [part] * array.shape[0], in_specs=[VMEM_SPEC], out_specs=[VMEM_SPEC] * array.shape[0]
    )(array)


def collect_kernel(chip_ref, *refs):
    for mask, ref in enumerate(refs[:-1]):
        refs[-1][chip_ref[0] ^ mask] = ref[...]


def collect(pieces, chip):
    return kernel_call(
        collect_kernel,
        jax.ShapeDtypeStruct((len(pieces), *pieces[0].shape), pieces[0].dtype),
        in_specs=[SMEM_SPEC] + [VMEM_SPEC] * len(pieces),
        out_specs=VMEM_SPEC,
    )(chip.reshape(1), *pieces)


def mlp_outputs_kernel(in_ref, up_ref, down_ref):
    up_ref[...] = in_ref[0, 0].astype(f32)
    down_ref[...] = in_ref[0, 1].astype(f32)


def mlp_outputs(grad, up_shape):
    pieces, _, rows, width = grad.shape
    hidden_local = pieces * rows
    if rows % 16:
        up, down = grad[:, 0].astype(f32), grad[:, 1].astype(f32)
    else:
        spec = pl.BlockSpec((rows, width), lambda index: (index, 0))
        out = jax.ShapeDtypeStruct((hidden_local, width), f32)
        up, down = kernel_call(
            mlp_outputs_kernel,
            [out, out],
            grid=(pieces,),
            in_specs=[pl.BlockSpec((1, 2, rows, width), lambda index: (index, 0, 0, 0))],
            out_specs=[spec, spec],
        )(grad)
    return up.reshape(up_shape), down.reshape(hidden_local, width)


def shards(
    tokens,
    condition,
    q_weight,
    q_bias,
    k_weight,
    v_weight,
    v_bias,
    o_weight,
    o_bias,
    up_weight,
    up_bias,
    down_weight,
    down_bias,
    ada_weight,
    ada_bias,
    out_grad,
    slot_clip,
    clip_patches,
):
    n_narrow = lax.axis_size("narrow")
    n_wide = lax.axis_size("wide")
    own_rows, width = tokens.shape
    clip_count = condition.shape[0]
    local = q_weight.shape[1]
    hidden_local = up_weight.shape[1]
    slot_count = slot_clip.shape[0]
    members = PATCH_HI // own_rows
    assert members * slot_count == n_narrow
    narrow_index = lax.axis_index("narrow")
    wide_index = lax.axis_index("wide")
    slot = narrow_index // members
    clip = slot_clip[slot]
    patches = clip_patches[clip].reshape(1)
    others = list(range(1, members))
    other_shards = list(range(1, slot_count))

    def member_of(at, step):
        return at // members * members + (at + step) % members

    def fetch_rows(array, step):
        return lax.ppermute(
            array, "narrow", [(member_of(at, step), at) for at in range(n_narrow)]
        )

    def send_rows(array, step):
        return lax.ppermute(
            array, "narrow", [(at, member_of(at, step)) for at in range(n_narrow)]
        )

    def fetch_shard(array, step):
        return lax.ppermute(
            array,
            "narrow",
            [((at + step * members) % n_narrow, at) for at in range(n_narrow)],
        )

    def send_shard(array, step):
        return lax.ppermute(
            array,
            "narrow",
            [(at, (at + step * members) % n_narrow) for at in range(n_narrow)],
        )

    def after(value, *earlier):
        return lax.optimization_barrier((value, *earlier))[0]

    def piece(weight):
        rows = weight.shape[0] // n_wide
        return lax.dynamic_slice_in_dim(weight, wide_index * rows, rows, 0)

    def gathered(pieces):
        return [lax.all_gather(each, "wide", axis=0, tiled=True) for each in pieces]

    def fetched(pack):
        return [fetch_shard(pack, step) for step in other_shards]

    own_pack = jnp.concatenate([q_weight.T, k_weight.T, v_weight.T, o_weight], axis=0)
    own_piece = piece(own_pack)
    attn_pieces = fetched(own_piece)
    bias_pack = jnp.concatenate([q_bias, jnp.zeros_like(q_bias), v_bias, up_bias])
    bias_packs = [bias_pack] + fetched(bias_pack)
    sent_tokens = after(tokens, own_piece)
    token_rows = [tokens] + [fetch_rows(sent_tokens, step) for step in others]

    cond_float = condition.astype(f32)
    silu_cond = jax.nn.silu(cond_float).astype(bf16)
    mod_part = (
        jnp.einsum("cd,dke->cke", silu_cond[slot_clip], ada_weight, preferred_element_type=f32)
        + ada_bias
    )
    mod_blocks = []
    for step in range(n_narrow):
        target = (narrow_index + step) % n_narrow
        block = lax.dynamic_index_in_dim(mod_part, target // members, 0, keepdims=False)
        if step:
            block = lax.ppermute(
                block, "narrow", [(at, (at + step) % n_narrow) for at in range(n_narrow)]
            )
        mod_blocks.append(block)
    mod_slot = jnp.roll(jnp.stack(mod_blocks[::-1]), narrow_index + 1, axis=0)
    modulation = mod_slot.transpose(1, 0, 2).reshape(6, width)

    packs = [own_pack]
    packs += gathered(
        [after(each, mod_part, token_rows[-1], *bias_packs[1:]) for each in attn_pieces]
    )
    qkv_biases = [pack[: 3 * local] for pack in bias_packs]
    up_biases = jnp.stack([pack[3 * local :] for pack in bias_packs]).reshape(slot_count, 1, -1)

    attn_in = modulated_rows(token_rows, modulation)
    qkv = [qkv_rows(attn_in, packs[0], qkv_biases[0])]

    flat_shape = (hidden_local, width)
    mlp_pack = jnp.concatenate([piece(up_weight.reshape(flat_shape)), piece(down_weight)], axis=1)
    mlp_pack = after(mlp_pack, token_rows[-1], modulation)
    mlp_pieces = fetched(mlp_pack)
    own_grad = after(out_grad, *mlp_pieces)
    grad_rows = [own_grad] + [fetch_rows(own_grad, step) for step in others]

    half_rows = max(own_rows // 2, BLOCK)
    halves_of = {block: own_rows // half_rows for block in others}
    halves_of[0] = 1
    attended = [{} for _ in range(slot_count)]
    lse = [{} for _ in range(slot_count)]
    attended_turned = [{} for _ in range(slot_count)]

    def attend(index, block, half, *earlier):
        rows = own_rows // halves_of[block]
        results = attention_forward(
            after(qkv[index], *earlier), patches, block * own_rows + half * rows, rows
        )
        for kept, result in zip((attended, attended_turned, lse), results):
            kept[index][block, half] = result
        return results[0]

    parts_of = [(block, half) for block in others for half in range(halves_of[block])]
    for part in parts_of:
        last_rows = attend(0, *part)
    mlp_packs = gathered([after(each, last_rows) for each in mlp_pieces])
    for index in other_shards:
        rows = after(attn_in, last_rows)
        qkv.append(qkv_rows(rows, packs[index], qkv_biases[index]))

    def branch_sum(rows, pack_refs):
        return sum(dot(each, ref[3 * local :]) for each, ref in zip(rows, pack_refs))

    zero_row = jnp.zeros((1, width), f32)
    def branch_part(part, kind):
        rows = [parts[part] for parts in attended]
        return row_call(
            lambda rows, vectors: ([branch_sum(rows, vectors[1:])], []), rows, [zero_row, *packs], [kind]
        )[0]

    arrived = {}
    earlier = []
    for part in parts_of:
        for index in other_shards:
            attend(index, *part, *earlier)
        earlier = [branch_part(part, bf16)]
        arrived[part] = send_rows(earlier[0], part[0])
    last_rows = attend(0, 0, 0, *earlier)
    for index in other_shards:
        last_rows = attend(index, 0, 0, last_rows, *grad_rows[1:])
    own_branch = branch_part((0, 0), f32)

    def joined(parts, axis=0):
        parts = list(parts)
        return parts[0] if len(parts) == 1 else jnp.concatenate(parts, axis=axis)

    def blocks_of(parts, axis):
        return [
            joined((parts[block, half] for half in range(halves_of[block])), axis)
            for block in range(members)
        ]

    lse = [blocks_of(parts, 1) for parts in lse]
    attended_turned = [
        [parts[block, half] for block in range(members) for half in range(halves_of[block])]
        for parts in attended_turned
    ]
    arrived = [
        joined(after(arrived[block, half], own_branch) for half in range(halves_of[block]))
        for block in others
    ]

    def middle_body(rows, vectors):
        token, *rest = [each.astype(f32) for each in rows]
        mod_ref, bias_ref = vectors
        branch = sum(rest[1:], rest[0]) + bias_ref[...].astype(f32)
        normed = normalize(token + mod_ref[2:3] * branch)[0]
        return [branch, normed * (1.0 + mod_ref[4:5]) + mod_ref[3:4]], []

    branch_one, mlp_own = row_call(
        middle_body,
        [tokens, own_branch, *arrived],
        [modulation, o_bias.reshape(1, width)],
        [f32, bf16],
    )

    mlp_rows = [mlp_own] + [fetch_rows(mlp_own, step) for step in others]
    ups, downs = [(up_weight, 0)], [(down_weight, 0)]
    for pack in mlp_packs:
        if hidden_local == width and hidden_local % HIDDEN_BLOCK == 0:
            ups.append((pack, 0))
            downs.append((pack, 1))
        else:
            ups.append((pack[:, :width].reshape(up_weight.shape), 0))
            downs.append((pack[:, width:], 0))
    hidden, d_pre, d_branch_two, d_mlp, branch_two, bias_sums_up = [], [], [], [], [], []
    for block in range(members):
        rows = after(mlp_rows[block], *d_mlp)
        results = feed_forward(
            rows, grad_rows[block], modulation, up_biases, ups, downs, bf16 if block else f32
        )
        for kept, result in zip((hidden, d_pre, d_branch_two, d_mlp, branch_two, bias_sums_up), results):
            kept.append(result)
    arrived = [send_rows(d_mlp[block], block) for block in others]
    grad_mlp_part = mlp_gradients(mlp_rows, d_branch_two, hidden, d_pre, n_wide)
    up_bias_sums = sum(bias_sums_up)[:slot_count]

    def d_middle_body(rows, vectors):
        token, branch, grad, *parts = [each.astype(f32) for each in rows]
        (mod_ref,) = vectors
        d_mlp_in = sum(parts[1:], parts[0])
        normed, inverse = normalize(token + mod_ref[2:3] * branch)
        d_middle = grad + norm_back(d_mlp_in * (1.0 + mod_ref[4:5]), normed, inverse)
        d_branch_one = (mod_ref[2:3] * d_middle).astype(bf16)
        terms = [d_middle * branch, d_mlp_in, d_mlp_in * normed, d_branch_one.astype(f32)]
        return [d_branch_one, d_middle], terms

    arrived = [after(part, grad_mlp_part) for part in arrived]
    d_branch_one, d_middle, middle_sums = row_call(
        d_middle_body, [tokens, branch_one, out_grad, d_mlp[0], *arrived], [modulation], [bf16, f32], 4
    )
    mlp_scattered = lax.psum_scatter(after(grad_mlp_part, *arrived), "wide", scatter_dimension=0, tiled=True)
    d_branch_rows = [d_branch_one] + [fetch_rows(d_branch_one, step) for step in others]

    assert n_wide & (n_wide - 1) == 0
    bits = n_wide.bit_length() - 1
    chips = n_wide // 2
    core, chip = wide_index % 2, wide_index // 2

    def wide_xor(array, mask):
        return lax.ppermute(array, "wide", [(at, at ^ mask) for at in range(n_wide)])

    def start_cores(part):
        keep, send = part
        return keep, wide_xor(send, 1)

    def end_cores(started):
        return split_pieces(*started, chip)

    def start_chips(pieces):
        return [pieces[0]] + [wide_xor(each, 2 * mask) for mask, each in enumerate(pieces[1:], 1)]

    shard_order = other_shards + [0]
    d_query = [[None] * members for _ in range(slot_count)]
    d_query_turned = [[None] * members for _ in range(slot_count)]
    d_kv, d_kv_turned = [None] * slot_count, [None] * slot_count
    grad_attn_part, attn_bias_sums = [None] * slot_count, [None] * slot_count

    def attn_gradients_of(index, *earlier):
        grad_attn_part[index], attn_bias_sums[index] = attn_gradients(
            attn_in,
            after(d_kv_turned[index], *earlier),
            d_query_turned[index],
            d_branch_rows,
            attended_turned[index],
            core,
            chips,
        )

    for block in range(members):
        last = block == members - 1
        for index in shard_order:
            d_query[index][block], d_query_turned[index][block], d_kv[index], *turned = (
                attention_backward(
                    qkv[index],
                    d_branch_rows[block],
                    packs[index],
                    lse[index][block],
                    patches,
                    d_kv[index],
                    block * own_rows,
                    last,
                )
            )
            if last:
                d_kv_turned[index] = turned[0]
                if index:
                    attn_gradients_of(index)
                    d_branch_rows[block] = after(d_branch_rows[block], grad_attn_part[index][0])
        if not last:
            d_branch_rows[block + 1] = after(d_branch_rows[block + 1], d_kv[0])

    def d_attn_sum(rows, pack_refs):
        total = 0.0
        for index, ref in enumerate(pack_refs):
            total = total + dot(rows[2 * index], ref[:local])
            total = total + dot(rows[2 * index + 1], ref[local : 3 * local])
        return total

    def d_rows_of(block):
        rows = []
        for index in range(slot_count):
            rows += [d_query[index][block], (d_kv[index], block * own_rows)]
        return rows

    cores_ended = [end_cores(start_cores(part)) for part in grad_attn_part[1:]]
    chips_started_of = {index: start_chips(cores_ended[index - 1]) for index in other_shards}
    mlp_scattered = after(mlp_scattered, d_kv[0])
    mlp_sent = cut(mlp_scattered.reshape(slot_count, 2, -1, width))
    mlp_arrived = [send_shard(mlp_sent[step], step) for step in other_shards]
    attn_gradients_of(0, *mlp_sent[1:], *(pieces[0] for pieces in cores_ended))
    d_kv[0] = after(d_kv[0], grad_attn_part[0][0])
    def d_attn_part(block, kind):
        return row_call(
            lambda rows, vectors: ([d_attn_sum(rows, vectors[1:])], []),
            d_rows_of(block),
            [zero_row, *packs],
            [kind],
        )[0]

    d_attn_parts = [d_attn_part(block, bf16) for block in others]
    arrived = [send_rows(part, block) for part, block in zip(d_attn_parts, others)]
    own_cores = start_cores(grad_attn_part[0])

    late_branch = [after(branch_two[block], *d_branch_rows[1:]) for block in others]
    arrived_two = [send_rows(part, block) for part, block in zip(late_branch, others)]
    arrived_two = [after(part, *d_attn_parts) for part in arrived_two]

    def out_body(rows, vectors):
        token, branch, grad, *parts = [each.astype(f32) for each in rows]
        mod_ref, bias_ref = vectors
        total = sum(parts[1:], parts[0]) + bias_ref[...].astype(f32)
        block_out = token + mod_ref[2:3] * branch + mod_ref[5:6] * total
        return [block_out], [grad * total, (mod_ref[5:6] * grad).astype(bf16).astype(f32)]

    block_out, out_sums = row_call(
        out_body,
        [tokens, branch_one, out_grad, branch_two[0], *arrived_two],
        [modulation, down_bias.reshape(1, width)],
        [bf16],
        2,
    )
    d_query[0][0] = after(d_query[0][0], block_out)
    own_d_attn = d_attn_part(0, f32)
    def end_body(rows, vectors):
        token, d_middle_rows, *parts = rows
        (mod_ref,) = vectors
        d_attn_in = sum([each.astype(f32) for each in parts[1:]], parts[0])
        normed, inverse = normalize(token.astype(f32))
        grad = d_middle_rows + norm_back(d_attn_in * (1.0 + mod_ref[1:2]), normed, inverse)
        return [grad], [d_attn_in, d_attn_in * normed]

    piece_sums = []
    for index in other_shards:
        own, *pieces = chips_started_of[index]
        piece_sums.append(add_arrays(own, *(after(each, own_d_attn) for each in pieces)))
    own_pieces = end_cores((own_cores[0], after(own_cores[1], *d_attn_parts)))
    chips_started = start_chips(own_pieces)
    arrived = [after(part, own_d_attn, own_pieces[0], *piece_sums) for part in arrived]
    grad_tokens, end_sums = row_call(
        end_body, [tokens, d_middle, own_d_attn, *arrived], [modulation], [f32], 2
    )

    sent = [send_shard(each, index) for index, each in zip(other_shards, piece_sums)]
    mlp_total = add_arrays(mlp_sent[0], *(after(each, own_d_attn) for each in mlp_arrived))

    own_sums = jnp.concatenate(
        [end_sums[0:2], middle_sums[0:3], out_sums[0:1], middle_sums[3:4], out_sums[1:2]]
    )
    bit = 1
    while bit < members:
        own_sums = own_sums + lax.ppermute(
            own_sums, "narrow", [(at, at ^ bit) for at in range(n_narrow)]
        )
        bit *= 2
    shard_parts = [
        jnp.concatenate([attn_bias_sums[step].reshape(-1), up_bias_sums[step]])
        for step in range(slot_count)
    ]
    slot_sums = [own_sums] + [fetch_shard(own_sums, step) for step in other_shards]
    shard_parts[1:] = [send_shard(shard_parts[step], step) for step in other_shards]
    total = add_arrays(*chips_started, *sent)

    grad_mlp = lax.all_gather(mlp_total, "wide", axis=0, tiled=False)
    grad_up_weight, grad_down_weight = mlp_outputs(grad_mlp, up_weight.shape)

    pieces = collect([total] + [wide_xor(total, 2 * mask) for mask in range(1, chips)], chip)
    flipped_pieces = wide_xor(pieces, 1)

    clip_ids = jnp.arange(clip_count, dtype=jnp.int32)
    d_mod_clips = jnp.zeros((clip_count, 6, local), f32)
    bias_sums = jnp.zeros((2, width), f32)
    shard_sum = jnp.zeros((3 * local + hidden_local,), f32)
    for step in range(slot_count):
        source_clip = slot_clip[(slot + step) % slot_count]
        one_hot = (clip_ids == source_clip).astype(f32)
        columns = lax.dynamic_slice_in_dim(slot_sums[step][:6], narrow_index * local, local, 1)
        d_mod_clips = d_mod_clips + one_hot[:, None, None] * columns
        bias_sums = bias_sums + slot_sums[step][6:]
        shard_sum = shard_sum + shard_parts[step]
    small = jnp.concatenate([d_mod_clips.reshape(-1), bias_sums.reshape(-1), shard_sum])
    for bit in range(bits):
        small = small + wide_xor(small, 1 << bit)
    grad_q_weight, grad_k_weight, grad_v_weight, grad_o_weight = attn_outputs(
        pieces, flipped_pieces, core
    )
    mod_size = clip_count * 6 * local
    d_modulation = small[:mod_size].reshape(clip_count, 6, local)
    grad_o_bias = small[mod_size : mod_size + width]
    grad_down_bias = small[mod_size + width : mod_size + 2 * width]
    shard_sum = small[mod_size + 2 * width :]
    grad_q_bias = shard_sum[:local]
    grad_v_bias = shard_sum[2 * local : 3 * local]
    grad_up_bias = shard_sum[3 * local :]

    silu_float = silu_cond.astype(f32)
    grad_ada_weight = jnp.einsum("cd,cke->dke", silu_float, d_modulation, precision=highest)
    grad_ada_bias = jnp.sum(d_modulation, axis=0)
    d_silu = jnp.einsum(
        "cke,dke->cd", d_modulation, ada_weight.astype(f32), precision=highest
    )
    bit = 1
    while bit < n_narrow:
        d_silu = d_silu + lax.ppermute(d_silu, "narrow", [(at, at ^ bit) for at in range(n_narrow)])
        bit *= 2
    grad_condition = jax.vjp(jax.nn.silu, cond_float)[1](d_silu)[0]
    return (
        block_out,
        grad_tokens,
        grad_condition,
        grad_q_weight,
        grad_q_bias,
        grad_k_weight,
        grad_v_weight,
        grad_v_bias,
        grad_o_weight,
        grad_o_bias,
        grad_up_weight,
        grad_up_bias,
        grad_down_weight,
        grad_down_bias,
        grad_ada_weight,
        grad_ada_bias,
    )


def solution(mesh):
    in_specs = (
        P(("wide", "narrow"), None),
        P(),
        P(None, "narrow"),
        P("narrow"),
        P(None, "narrow"),
        P(None, "narrow"),
        P("narrow"),
        P("narrow", None),
        P(),
        P(None, "narrow"),
        P("narrow"),
        P("narrow", None),
        P(),
        P(None, None, "narrow"),
        P(None, "narrow"),
        P(("wide", "narrow"), None),
        P("wide"),
        P(),
    )
    out_specs = (
        P(("wide", "narrow"), None),
        P(("wide", "narrow"), None),
        P(),
        P(None, "narrow"),
        P("narrow"),
        P(None, "narrow"),
        P(None, "narrow"),
        P("narrow"),
        P("narrow", None),
        P(),
        P(None, "narrow"),
        P("narrow"),
        P("narrow", None),
        P(),
        P(None, None, "narrow"),
        P(None, "narrow"),
    )
    return jax.shard_map(shards, mesh=mesh, in_specs=in_specs, out_specs=out_specs, check_vma=False)
```

time: 1700 us -> 462 us (0.27)
  waiting for transfers between devices: 1120 us -> 116 us
  matrix products: 257 us -> 12.4 us
  Pallas kernels: 0 us -> 218 us
  blocking collectives: 135 us -> 0 us
  other arithmetic: 92 us -> 6.29 us
  starting transfers between devices: 0.58 us -> 41 us
  local copies, waits for them, and re-layouts: 79.4 us -> 42.4 us
    reduce_scatter x4 -> x1, waiting for transfers between devices: 509 us -> 9.11 us  [shards(): lax.psum_scatter(after(grad_mlp_part, *arrived), 'wide', scatter_dimensio...]
    all_gather x4 -> x3, waiting for transfers between devices: 344 us -> 0.02 us  [the longest x2 0.02 us: gathered(): return [lax.all_gather(each, 'wide', axis=0, tiled=True) for each in pieces]]
    psum x2 -> x0, waiting for transfers between devices: 263 us -> none  [the longest x1 183 us: shards(): lax.psum((grad_q_weight, grad_q_bias, grad_k_weight, grad_v_weight, grad_...]
    dot_general x28 -> x2, matrix products: 249 us -> 6.86 us  [the longest x1 3.45 us: shards(): jnp.einsum('cd,dke->cke', silu_cond[slot_clip], ada_weight, preferred_ele...]
    pallas_call x0 -> x36, Pallas kernels: none -> 218 us  [the longest x2 46.2 us: feed_forward(): kernel_call(functools.partial(feed_forward_kernel, sum_type, shard_count)...]
    ppermute x0 -> x37, waiting for transfers between devices: none -> 106 us  [the longest x4 43.5 us: fetch_shard(): lax.ppermute(array, 'narrow', [((at + step * members) % n_narrow, at) for...]
    all_gather x1 -> x0, blocking collectives: 90.4 us -> none  [shards(): modulation = lax.all_gather(mod_part, 'narrow', axis=2, tiled=True)]
    psum x2 -> x0, blocking collectives: 44.4 us -> none  [the longest x1 24.2 us: shards(): lax.psum((grad_q_weight, grad_q_bias, grad_k_weight, grad_v_weight, grad_...]
  transfers between devices with their start and end apart: 10 -> 41, of which waited for: 10 -> 20; matrix products, arithmetic and copies ran while one was open for 6% -> 5% of each run, Pallas kernels for 0% -> 42%
where the time goes in v1:
time: 462 us; the launch traced here: 453 us
  Pallas kernels  218 us (47%)
  waiting for transfers between devices  116 us (25%)
  local copies, waits for them, and re-layouts  42.4 us (9%)
  starting transfers between devices  41 us (9%)
  between operations  17.2 us (4%)
  matrix products  12.4 us (3%)
  other arithmetic  6.29 us (1%)
    pallas_call x2, Pallas kernels, feed_forward(): kernel_call(functools.partial(feed_forward_kernel, sum_type, shard_count)...  46.2 us
    pallas_call x4, Pallas kernels, attention_backward(): kernel_call(functools.partial(attention_backward_kernel, first_row, first...  46.1 us
    ppermute x4, waiting for transfers between devices, fetch_shard(): lax.ppermute(array, 'narrow', [((at + step * members) % n_narrow, at) for...  43.5 us
    pallas_call x9, Pallas kernels, row_call(): kernel_call(kernel, outs, grid=(rows // step_rows,), in_specs=[pl.BlockSp...  40.6 us
    unnamed x167, local copies, waits for them, and re-layouts  37.1 us
    ppermute x15, waiting for transfers between devices, wide_xor(): lax.ppermute(array, 'wide', [(at, at ^ mask) for at in range(n_wide)])  30.9 us
    pallas_call x6, Pallas kernels, attention_forward(): kernel_call(functools.partial(attention_forward_kernel, first_row), (jax....  23.3 us
    ppermute x5, waiting for transfers between devices, send_rows(): lax.ppermute(array, 'narrow', [(at, member_of(at, step)) for at in range(...  20.7 us
  transfers between devices with their start and end apart: 41, of which 20 were waited for; matrix products, arithmetic and copies ran while one was open for 5% of the time, Pallas kernels for 42%

profile of v1, /device:TPU:0, one launch (start us, length us, event | category | flops | bytes accessed | tf_op | source)
XLA Modules:
  0.0 453.0 jit_solution(231850336459384830)
XLA Ops:
  19.5 25.5 %collective-permute-done.5 = bf16[2016]{0:T(1024)(128)(2,1)S(1)} collective-permute-done((bf16[2016]{0:T(1024)(128)(2,1)S(1)}, bf16[2016]{0:T(1024)(128)(2,1)S(1)}, u32[]{:S(2)}, u32[]{:S(2)}) %collective-permute-start.5) | collective-permute-done | bytes 4064 | tf_op jit(solution)/shard_map/ppermute | solution.py:631
  46.1 3.8 collective-permute-start.1
  63.3 6.1 %shard_map.298.qkv_ref.refs_1_ = bf16[1024,864]{1,0:T(8,128)(2,1)S(1)} custom-call(bf16[1024,1152]{1,0:T(8,128)(2,1)S(1)} %bitcast.39, bf16[1152,1152]{1,0:T(8,128)(2,1)} %copy-done, bf16[1,864]{1,0:T(2,128)(2,1)S(1)} %reshape.101.bias_ref), custom_call_target="tpu_custom_call" | custom-call | bytes 1024 | tf_op jit(solution)/shard_map/pallas_call | solution.py:146
  72.5 13.2 %collective-permute-done.6 = bf16[144,2304]{1,0:T(8,128)(2,1)S(1)} collective-permute-done((bf16[144,2304]{1,0:T(8,128)(2,1)}, bf16[144,2304]{1,0:T(8,128)(2,1)S(1)}, u32[]{:S(2)}, u32[]{:S(2)}) %collective-permute-start.6) | collective-permute-done | bytes 663584 | tf_op jit(solution)/shard_map/ppermute | solution.py:631
  92.1 5.7 %shard_map.300.qkv_ref.refs_1_ = bf16[1024,864]{1,0:T(8,128)(2,1)S(1)} custom-call(bf16[1024,1152]{1,0:T(8,128)(2,1)S(1)} %bitcast.42, bf16[1152,1152]{1,0:T(8,128)(2,1)} %all-gather.5.cloned.1.call-done.pack_ref.refs_4_.refs_3_.refs_6_, bf16[1,864]{1,0:T(2,128)(2,1)S(1)} %reshape.102.bias_ref), custom_call_target="tpu_custom_call" | custom-call | bytes 1024 | tf_op jit(solution)/shard_map/pallas_call | solution.py:146
  111.6 5.1 %shard_map.306 = (bf16[512,288]{1,0:T(8,128)(2,1)S(1)}, bf16[288,512]{1,0:T(8,128)(2,1)S(1)}, f32[4,512]{1,0:T(4,128)S(1)}) custom-call(s32[1]{0:T(128)} %dynamic_slice.45.patches_ref.refs_0_, bf16[1024,864]{1,0:T(8,128)(2,1)S(1)} %copy-done.3), custom_call_target="tpu_custom_call" | custom-call | bytes 1024 | tf_op jit(solution)/shard_map/pallas_call | solution.py:221
  116.6 6.0 %shard_map.307 = (bf16[512,288]{1,0:T(8,128)(2,1)S(1)}, bf16[288,512]{1,0:T(8,128)(2,1)S(1)}, f32[4,512]{1,0:T(4,128)S(1)}) custom-call(s32[1]{0:T(128)} %dynamic_slice.45.patches_ref.refs_0_, bf16[1024,864]{1,0:T(8,128)(2,1)S(1)} %shard_map.300.qkv_ref.refs_1_), custom_call_target="tpu_custom_call" | custom-call | bytes 1024 | tf_op jit(solution)/shard_map/pallas_call | solution.py:221
  128.4 11.7 %collective-permute-done.8 = bf16[256,1152]{1,0:T(8,128)(2,1)S(1)} collective-permute-done((bf16[256,1152]{1,0:T(8,128)(2,1)S(1)}, bf16[256,1152]{1,0:T(8,128)(2,1)S(1)}, u32[]{:S(2)}, u32[]{:S(2)}) %collective-permute-start.8) | collective-permute-done | bytes 589856 | tf_op jit(solution)/shard_map/ppermute | solution.py:626
  144.7 23.4 %shard_map.310 = (bf16[2,512,1152]{2,1,0:T(8,128)(2,1)S(1)}, bf16[2,512,1152]{2,1,0:T(8,128)(2,1)}, bf16[512,1152]{1,0:T(8,128)(2,1)S(1)}, f32[512,1152]{1,0:T(8...) custom-call(bf16[512,1152]{1,0:T(8,128)(2,1)S(1)} %get-tuple-element.136.refs_0_, bf16[512,1152]{1,0:T(8,128)(2,1)} %refs_2_.3, ...), custom_call_target="tpu_custom_call" | custom-call | bytes 1024 | tf_op jit(solution)/shard_map/pallas_call | solution.py:359
  171.3 22.8 %shard_map.311 = (bf16[2,512,1152]{2,1,0:T(8,128)(2,1)}, bf16[2,512,1152]{2,1,0:T(8,128)(2,1)}, bf16[512,1152]{1,0:T(8,128)(2,1)S(1)}, bf16[512,1152]{1,0:T(8,12...) custom-call(bf16[512,1152]{1,0:T(8,128)(2,1)S(1)} %collective-permute-done.10.refs_0_.refs_1_, ...), custom_call_target="tpu_custom_call" | custom-call | bytes 1024 | tf_op jit(solution)/shard_map/pallas_call | solution.py:359
  195.3 17.1 %shard_map.312 = bf16[8,4,144,1152]{3,2,1,0:T(8,128)(2,1)} custom-call(bf16[512,1152]{1,0:T(8,128)(2,1)S(1)} %get-tuple-element.136.refs_0_, bf16[512,1152]{1,0:T(8,128)(2,1)S(1)} %collective-permute-done.10.refs_0_.refs_1_, bf16[512,1152]{1,0:T(8,128)(2,1)S(1)} %get-tuple-element.143.refs_2_, bf16[512,1152]{1,0:T(8,128)(2,1)S(1)} %get-tuple-element.144.refs_3_, ...), custom_call_target="tpu_custom_call" | custom-call | bytes 1024 | tf_op jit(solution)/shard_map/pallas_call | solution.py:411
  212.4 8.8 %collective-permute-done.11.refs_4_ = bf16[512,1152]{1,0:T(8,128)(2,1)} collective-permute-done((bf16[512,1152]{1,0:T(8,128)(2,1)}, bf16[512,1152]{1,0:T(8,128)(2,1)}, u32[]{:S(2)}, u32[]{:S(2)}) %collective-permute-start.11) | collective-permute-done | bytes 1179680 | tf_op jit(solution)/shard_map/ppermute | solution.py:626
  221.2 6.4 %shard_map.313 = (bf16[512,1152]{1,0:T(8,128)(2,1)}, f32[512,1152]{1,0:T(8,128)}, f32[8,1152]{1,0:T(8,128)S(1)}) custom-call(bf16[512,1152]{1,0:T(8,128)(2,1)} %refs_0_.9, f32[512,1152]{1,0:T(8,128)} %copy-done.9, bf16[512,1152]{1,0:T(8,128)(2,1)} %refs_2_.3, f32[512,1152]{1,0:T(8,128)} %get-tuple-element.139.refs_3_, ...), custom_call_target="tpu_custom_call" | custom-call | bytes 1024 | tf_op jit(solution)/shard_map/pallas_call | solution.py:103
  229.2 12.0 %shard_map.314 = (bf16[512,288]{1,0:T(8,128)(2,1)S(1)}, bf16[288,512]{1,0:T(8,128)(2,1)S(1)}, f32[576,1024]{1,0:T(8,128)S(1)}) custom-call(s32[1]{0:T(128)} %dynamic_slice.45.patches_ref.refs_0_, bf16[1024,864]{1,0:T(8,128)(2,1)S(1)} %copy-done.4, bf16[512,1152]{1,0:T(8,128)(2,1)} %get-tuple-element.150.refs_2_.refs_5_, bf16[1152,1152]{1,0:T(8,128)(2,1)} %copy-done, ...), custom_call_target="tpu_custom_call" | custom-call | bytes 1024 | tf_op jit(solution)/shard_map/pallas_call | solution.py:296
  244.0 10.5 %shard_map.315 = (bf16[512,288]{1,0:T(8,128)(2,1)S(1)}, bf16[288,512]{1,0:T(8,128)(2,1)S(1)}, f32[576,1024]{1,0:T(8,128)S(1)}) custom-call(s32[1]{0:T(128)} %dynamic_slice.45.patches_ref.refs_0_, bf16[1024,864]{1,0:T(8,128)(2,1)S(1)} %copy-done.6, bf16[512,1152]{1,0:T(8,128)(2,1)} %get-tuple-element.150.refs_2_.refs_5_, ...), custom_call_target="tpu_custom_call" | custom-call | bytes 1024 | tf_op jit(solution)/shard_map/pallas_call | solution.py:296
  256.8 11.7 %shard_map.316 = (bf16[512,288]{1,0:T(8,128)(2,1)S(1)}, bf16[288,512]{1,0:T(8,128)(2,1)S(1)}, bf16[1024,576]{1,0:T(8,128)(2,1)S(1)}, bf16[576,1024]{1,0:T(8,128)(2,1)S(1)}) custom-call(s32[1]{0:T(128)} %dynamic_slice.45.patches_ref.refs_0_, bf16[1024,864]{1,0:T(8,128)(2,1)S(1)} %copy-done.6, bf16[512,1152]{1,0:T(8,128)(2,1)S(1)} %collective-permute-done.12.refs_2_.refs_6_, ...), custom_call_target="tpu_custom_call" | custom-call | bytes 1024 | tf_op jit(solution)/shard_map/pallas_call | solution.py:296
  270.4 6.8 %shard_map.317 = (bf16[4,144,1152]{2,1,0:T(8,128)(2,1)}, bf16[4,144,1152]{2,1,0:T(8,128)(2,1)}, f32[864,1]{1,0:T(8,128)S(1)}) custom-call(s32[1]{0:T(128)} %bitcast.8.refs_0_.core_ref, bf16[1024,1152]{1,0:T(8,128)(2,1)} %bitcast.40, bf16[576,1024]{1,0:T(8,128)(2,1)S(1)} %get-tuple-element.158.refs_2_, bf16[288,512]{1,0:T(8,128)(2,1)S(1)} %get-tuple-element.159.refs_3_, ...), custom_call_target="tpu_custom_call" | custom-call | bytes 1024 | tf_op jit(solution)/shard_map/pallas_call | solution.py:463
  278.3 11.8 %shard_map.318 = (bf16[512,288]{1,0:T(8,128)(2,1)S(1)}, bf16[288,512]{1,0:T(8,128)(2,1)S(1)}, bf16[1024,576]{1,0:T(8,128)(2,1)S(1)}, bf16[576,1024]{1,0:T(8,128)(2,1)S(1)}) custom-call(s32[1]{0:T(128)} %dynamic_slice.45.patches_ref.refs_0_, bf16[1024,864]{1,0:T(8,128)(2,1)S(1)} %copy-done.4, bf16[512,1152]{1,0:T(8,128)(2,1)S(1)} %collective-permute-done.12.refs_2_.refs_6_, ...), custom_call_target="tpu_custom_call" | custom-call | bytes 1024 | tf_op jit(solution)/shard_map/pallas_call | solution.py:296
  293.8 9.1 %reduce-scatter.2.cloned.1.call-done = bf16[1,4,144,1152]{3,2,1,0:T(8,128)(2,1)} async-done(((bf16[8,4,144,1152]{3,2,1,0:T(8,128)(2,1)}), bf16[1,4,144,1152]{3,2,1,0:T(8,128)(2,1)}) %reduce-scatter.2.cloned.1.call-update) | async-done | bytes 1327120 | tf_op jit(solution)/shard_map/reduce_scatter | solution.py:815
  316.7 7.1 %shard_map.321 = (bf16[4,144,1152]{2,1,0:T(8,128)(2,1)}, bf16[4,144,1152]{2,1,0:T(8,128)(2,1)}, f32[864,1]{1,0:T(8,128)S(1)}) custom-call(s32[1]{0:T(128)} %bitcast.8.refs_0_.core_ref, bf16[1024,1152]{1,0:T(8,128)(2,1)} %bitcast.41, bf16[576,1024]{1,0:T(8,128)(2,1)S(1)} %copy-done.26, bf16[288,512]{1,0:T(8,128)(2,1)S(1)} %copy-done.50, ...), custom_call_target="tpu_custom_call" | custom-call | bytes 1024 | tf_op jit(solution)/shard_map/pallas_call | solution.py:463
  323.9 7.4 %shard_map.322 = bf16[512,1152]{1,0:T(8,128)(2,1)} custom-call(bf16[512,288]{1,0:T(8,128)(2,1)S(1)} %copy-done.34, bf16[1024,576]{1,0:T(8,128)(2,1)S(1)} %copy-done.17, bf16[512,288]{1,0:T(8,128)(2,1)S(1)} %copy-done.32, bf16[1024,576]{1,0:T(8,128)(2,1)S(1)} %copy-done.15, f32[1,1152]{1,0:T(1,128)S(1)} %broadcast_in_dim.16.refs_2_.refs_4_, ...), custom_call_target="tpu_custom_call" | custom-call | bytes 1024 | tf_op jit(solution)/shard_map/pallas_call | solution.py:103
  331.3 4.1 shard_map.323
  335.4 6.2 %shard_map.324.refs_2_ = f32[512,1152]{1,0:T(8,128)S(1)} custom-call(bf16[512,288]{1,0:T(8,128)(2,1)S(1)} %copy-done.36, bf16[1024,576]{1,0:T(8,128)(2,1)S(1)} %copy-done.17, bf16[512,288]{1,0:T(8,128)(2,1)S(1)} %copy-done.38, bf16[1024,576]{1,0:T(8,128)(2,1)S(1)} %copy-done.15, f32[1,1152]{1,0:T(1,128)S(1)} %broadcast_in_dim.16.refs_2_.refs_4_, ...), custom_call_target="tpu_custom_call" | custom-call | bytes 1024 | tf_op jit(solution)/shard_map/pallas_call | solution.py:103
  351.9 10.0 %collective-permute-done.19.refs_3_ = bf16[144,1152]{1,0:T(8,128)(2,1)S(1)} collective-permute-done((bf16[144,1152]{1,0:T(8,128)(2,1)S(1)}, bf16[144,1152]{1,0:T(8,128)(2,1)S(1)}, u32[]{:S(2)}, u32[]{:S(2)}) %collective-permute-start.19) | collective-permute-done | bytes 331808 | tf_op jit(solution)/shard_map/ppermute | solution.py:824
  365.1 6.9 %collective-permute-done.18.refs_2_ = bf16[144,1152]{1,0:T(8,128)(2,1)} collective-permute-done((bf16[144,1152]{1,0:T(8,128)(2,1)}, bf16[144,1152]{1,0:T(8,128)(2,1)}, u32[]{:S(2)}, u32[]{:S(2)}) %collective-permute-start.18) | collective-permute-done | bytes 331808 | tf_op jit(solution)/shard_map/ppermute | solution.py:824
  378.7 5.1 %shard_map.327 = (f32[512,1152]{1,0:T(8,128)}, f32[8,1152]{1,0:T(8,128)S(1)}) custom-call(bf16[512,1152]{1,0:T(8,128)(2,1)} %refs_0_.9, f32[512,1152]{1,0:T(8,128)S(1)} %copy-done.19, f32[512,1152]{1,0:T(8,128)} %copy-done.11, bf16[512,1152]{1,0:T(8,128)(2,1)} %collective-permute-done.15.refs_3_, f32[6,1152]{1,0:T(8,128)S(1)} %reshape.99.refs_2_.refs_3_.refs_5_.refs_4_), custom_call_target="tpu_custom_call" | custom-call | bytes 1024 | tf_op jit(solution)/shard_map/pallas_call | solution.py:103
  388.1 4.7 %collective-permute-done.20 = f32[8,1152]{1,0:T(8,128)S(1)} collective-permute-done((f32[8,1152]{1,0:T(8,128)S(1)}, f32[8,1152]{1,0:T(8,128)S(1)}, u32[]{:S(2)}, u32[]{:S(2)}) %collective-permute-start.20) | collective-permute-done | bytes 36896 | tf_op jit(solution)/shard_map/ppermute | solution.py:955
  393.0 4.8 %collective-permute-done.21 = f32[8,1152]{1,0:T(8,128)S(1)} collective-permute-done((f32[8,1152]{1,0:T(8,128)S(1)}, f32[8,1152]{1,0:T(8,128)S(1)}, u32[]{:S(2)}, u32[]{:S(2)}) %collective-permute-start.21) | collective-permute-done | bytes 36896 | tf_op jit(solution)/shard_map/ppermute | solution.py:631
  400.2 5.2 %collective-permute-done.24 = f32[12960]{0:T(1024)S(1)} collective-permute-done((f32[12960]{0:T(1024)S(1)}, f32[12960]{0:T(1024)S(1)}, u32[]{:S(2)}, u32[]{:S(2)}) %collective-permute-start.24) | collective-permute-done | bytes 51872 | tf_op jit(solution)/shard_map/ppermute | solution.py:824
  420.0 4.3 collective-permute-done.33.refs_2_
  424.5 5.5 %fusion = f32[1152,6,288]{0,2,1:T(8,128)} fusion(f32[5,6,288]{2,1,0:T(8,128)S(1)} %reshape.112, bf16[5,1152]{1,0:T(8,128)(2,1)S(1)} %copy-done.73), kind=kOutput, calls=%fused_computation.6 | convolution fusion | flops 119473920 | bytes 8008704 | tf_op jit(solution)/shard_map/cd,cke->dke/dot_general | solution.py:1000
  441.4 4.8 %shard_map.332 = (f32[1152,1152]{1,0:T(8,128)}, f32[1152,1152]{1,0:T(8,128)}) custom-call(bf16[8,2,144,1152]{3,2,1,0:T(8,128)(2,1)S(1)} %bitcast.43), custom_call_target="tpu_custom_call" | custom-call | bytes 1024 | tf_op jit(solution)/shard_map/pallas_call | solution.py:570
  (325 shorter events, 142.1 us)
Async XLA Ops:
  7.2 83.2 %all-gather.5.cloned.1.call-start = ((), (), s32[]{:S(2)}) async-start(), calls=%async_computation.1 | async-start | bytes 2985984 | tf_op jit(solution)/shard_map/all_gather | solution.py:652
  9.3 36.6 %collective-permute-start = (bf16[512,1152]{1,0:T(8,128)(2,1)}, bf16[512,1152]{1,0:T(8,128)(2,1)}, u32[]{:S(2)}, u32[]{:S(2)}) collective-permute-start(bf16[512,1152]{1,0:T(8,128)(2,1)} %refs_0_.9), channel_id=1, source_target_pairs={{1,0},{0,1},{3,2},{2,3},{5,4},{4,5},{7,6},{6,7},{9,8},{8,9},{11,10... | collective-permute-start | bytes 3538952 | tf_op jit(solution)/shard_map/ppermute | solution.py:621
  12.4 32.6 %collective-permute-start.4 = (bf16[144,1152]{1,0:T(8,128)(2,1)S(1)}, bf16[144,1152]{1,0:T(8,128)(2,1)S(1)}, u32[]{:S(2)}, u32[]{:S(2)}) collective-permute-start(bf16[144,1152]{1,0:T(8,128)(2,1)S(1)} %constant_dynamic-slice_fusion.8), channel_id=1, source_target_pairs={{2,0},{3,1},{0,2},{1,3},{6,4},{7,5},{4,6},{5,7},{10,8},{11,9},{8,1... | collective-permute-start | bytes 995336 | tf_op jit(solution)/shard_map/ppermute | solution.py:631
  15.1 29.9 %collective-permute-start.5 = (bf16[2016]{0:T(1024)(128)(2,1)S(1)}, bf16[2016]{0:T(1024)(128)(2,1)S(1)}, u32[]{:S(2)}, u32[]{:S(2)}) collective-permute-start(bf16[2016]{0:T(1024)(128)(2,1)S(1)} %concatenate.41), channel_id=1, source_target_pairs={{2,0},{3,1},{0,2},{1,3},{6,4},{7,5},{4,6},{5,7},{10,8},{11,9},{8,1... | collective-permute-start | bytes 12104 | tf_op jit(solution)/shard_map/ppermute | solution.py:631
  45.9 98.8 %all-gather.7.cloned.1.call-start = ((), (), s32[]{:S(2)}) async-start(), calls=%async_computation.2 | async-start | bytes 5971968 | tf_op jit(solution)/shard_map/all_gather | solution.py:652
  56.8 28.9 %collective-permute-start.6 = (bf16[144,2304]{1,0:T(8,128)(2,1)}, bf16[144,2304]{1,0:T(8,128)(2,1)S(1)}, u32[]{:S(2)}, u32[]{:S(2)}) collective-permute-start(bf16[144,2304]{1,0:T(8,128)(2,1)} %pad_maximum_fusion.2), channel_id=1, source_target_pairs={{2,0},{3,1},{0,2},{1,3},{6,4},{7,5},{4,6},{5,7},{10,8},{11,9},{8,1... | collective-permute-start | bytes 1990664 | tf_op jit(solution)/shard_map/ppermute | solution.py:631
  86.6 216.3 %reduce-scatter.2.cloned.1.call-start = ((), (), s32[]{:S(2)}) async-start(), calls=%async_computation.3 | async-start | bytes 11943936 | tf_op jit(solution)/shard_map/reduce_scatter | solution.py:815
  86.6 30.0 %collective-permute-start.7 = (bf16[512,1152]{1,0:T(8,128)(2,1)}, bf16[512,1152]{1,0:T(8,128)(2,1)}, u32[]{:S(2)}, u32[]{:S(2)}) collective-permute-start(bf16[512,1152]{1,0:T(8,128)(2,1)} %refs_2_.3), channel_id=1, source_target_pairs={{1,0},{0,1},{3,2},{2,3},{5,4},{4,5},{7,6},{6,7},{9,8},{8,9},{11,10... | collective-permute-start | bytes 3538952 | tf_op jit(solution)/shard_map/ppermute | solution.py:621
  109.4 19.0 %collective-permute-start.9 = (bf16[256,1152]{1,0:T(8,128)(2,1)S(1)}, bf16[256,1152]{1,0:T(8,128)(2,1)S(1)}, u32[]{:S(2)}, u32[]{:S(2)}) collective-permute-start(bf16[256,1152]{1,0:T(8,128)(2,1)S(1)} %shard_map.305), channel_id=1, source_target_pairs={{0,1},{1,0},{2,3},{3,2},{4,5},{5,4},{6,7},{7,6},{8,9},{9,8},{10,11... | collective-permute-start | bytes 1769480 | tf_op jit(solution)/shard_map/ppermute | solution.py:626
  111.5 28.6 %collective-permute-start.8 = (bf16[256,1152]{1,0:T(8,128)(2,1)S(1)}, bf16[256,1152]{1,0:T(8,128)(2,1)S(1)}, u32[]{:S(2)}, u32[]{:S(2)}) collective-permute-start(bf16[256,1152]{1,0:T(8,128)(2,1)S(1)} %shard_map.303), channel_id=1, source_target_pairs={{0,1},{1,0},{2,3},{3,2},{4,5},{5,4},{6,7},{7,6},{8,9},{9,8},{10,11... | collective-permute-start | bytes 1769480 | tf_op jit(solution)/shard_map/ppermute | solution.py:626
  144.2 27.0 %collective-permute-start.10 = (bf16[512,1152]{1,0:T(8,128)(2,1)S(1)}, bf16[512,1152]{1,0:T(8,128)(2,1)S(1)}, u32[]{:S(2)}, u32[]{:S(2)}) collective-permute-start(bf16[512,1152]{1,0:T(8,128)(2,1)S(1)} %get-tuple-element.136.refs_0_), channel_id=1, source_target_pairs={{1,0},{0,1},{3,2},{2,3},{5,4},{4,5},{7,6},{6,7},{9,8},{8,9},{11,10... | collective-permute-start | bytes 3538952 | tf_op jit(solution)/shard_map/ppermute | solution.py:621
  194.7 26.4 %collective-permute-start.11 = (bf16[512,1152]{1,0:T(8,128)(2,1)}, bf16[512,1152]{1,0:T(8,128)(2,1)}, u32[]{:S(2)}, u32[]{:S(2)}) collective-permute-start(bf16[512,1152]{1,0:T(8,128)(2,1)} %get-tuple-element.142), channel_id=1, source_target_pairs={{0,1},{1,0},{2,3},{3,2},{4,5},{5,4},{6,7},{7,6},{8,9},{9,8},{10,11... | collective-permute-start | bytes 3538952 | tf_op jit(solution)/shard_map/ppermute | solution.py:626
  221.2 217.7 %all-gather.9.cloned.1.call-start = ((), (), s32[]{:S(2)}) async-start(), calls=%async_computation.4 | async-start | bytes 5971968 | tf_op jit(solution)/shard_map/all_gather | solution.py:967
  228.2 28.6 %collective-permute-start.12 = (bf16[512,1152]{1,0:T(8,128)(2,1)}, bf16[512,1152]{1,0:T(8,128)(2,1)S(1)}, u32[]{:S(2)}, u32[]{:S(2)}) collective-permute-start(bf16[512,1152]{1,0:T(8,128)(2,1)} %get-tuple-element.150.refs_2_.refs_5_), channel_id=1, source_target_pairs={{1,0},{0,1},{3,2},{2,3},{5,4},{4,5},{7,6},{6,7},{9,8},{8,9},{11,10... | collective-permute-start | bytes 3538952 | tf_op jit(solution)/shard_map/ppermute | solution.py:621
  277.2 31.2 %collective-permute-start.14 = (bf16[4,144,1152]{2,1,0:T(8,128)(2,1)}, bf16[4,144,1152]{2,1,0:T(8,128)(2,1)}, u32[]{:S(2)}, u32[]{:S(2)}) collective-permute-start(bf16[4,144,1152]{2,1,0:T(8,128)(2,1)} %get-tuple-element.175), channel_id=1, source_target_pairs={{0,4},{4,0},{8,12},{12,8},{16,20},{20,16},{24,28},{28,24},{1,5},{5... | collective-permute-start | bytes 3981320 | tf_op jit(solution)/shard_map/ppermute | solution.py:824
  277.2 54.1 %collective-permute-start.13 = (bf16[512,1152]{1,0:T(8,128)(2,1)}, bf16[512,1152]{1,0:T(8,128)(2,1)}, u32[]{:S(2)}, u32[]{:S(2)}) collective-permute-start(bf16[512,1152]{1,0:T(8,128)(2,1)} %get-tuple-element.166), channel_id=1, source_target_pairs={{0,1},{1,0},{2,3},{3,2},{4,5},{5,4},{6,7},{7,6},{8,9},{9,8},{10,11... | collective-permute-start | bytes 3538952 | tf_op jit(solution)/shard_map/ppermute | solution.py:626
  306.0 37.1 %collective-permute-start.36 = (bf16[2,144,1152]{2,1,0:T(8,128)(2,1)}, bf16[2,144,1152]{2,1,0:T(8,128)(2,1)}, u32[]{:S(2)}, u32[]{:S(2)}) collective-permute-start(bf16[2,144,1152]{2,1,0:T(8,128)(2,1)} %get-tuple-element.174), channel_id=1, source_target_pairs={{0,2},{1,3},{2,0},{3,1},{4,6},{5,7},{6,4},{7,5},{8,10},{9,11},{10,... | collective-permute-start | bytes 1990664 | tf_op jit(solution)/shard_map/ppermute | solution.py:638
  345.3 30.4 %collective-permute-start.16 = (bf16[4,144,1152]{2,1,0:T(8,128)(2,1)}, bf16[4,144,1152]{2,1,0:T(8,128)(2,1)}, u32[]{:S(2)}, u32[]{:S(2)}) collective-permute-start(bf16[4,144,1152]{2,1,0:T(8,128)(2,1)} %get-tuple-element.193), channel_id=1, source_target_pairs={{0,4},{4,0},{8,12},{12,8},{16,20},{20,16},{24,28},{28,24},{1,5},{5... | collective-permute-start | bytes 3981320 | tf_op jit(solution)/shard_map/ppermute | solution.py:824
  345.4 33.3 %collective-permute-start.15 = (bf16[512,1152]{1,0:T(8,128)(2,1)}, bf16[512,1152]{1,0:T(8,128)(2,1)}, u32[]{:S(2)}, u32[]{:S(2)}) collective-permute-start(bf16[512,1152]{1,0:T(8,128)(2,1)} %shard_map.322), channel_id=1, source_target_pairs={{0,1},{1,0},{2,3},{3,2},{4,5},{5,4},{6,7},{7,6},{8,9},{9,8},{10,11... | collective-permute-start | bytes 3538952 | tf_op jit(solution)/shard_map/ppermute | solution.py:626
  346.9 15.1 %collective-permute-start.19 = (bf16[144,1152]{1,0:T(8,128)(2,1)S(1)}, bf16[144,1152]{1,0:T(8,128)(2,1)S(1)}, u32[]{:S(2)}, u32[]{:S(2)}) collective-permute-start(bf16[144,1152]{1,0:T(8,128)(2,1)S(1)} %copy-done.66), channel_id=1, source_target_pairs={{0,24},{4,28},{8,16},{12,20},{16,8},{20,12},{24,0},{28,4},{1,25},{... | collective-permute-start | bytes 995336 | tf_op jit(solution)/shard_map/ppermute | solution.py:824
  350.1 34.5 %collective-permute-start.22 = (f32[2016]{0:T(1024)S(1)}, f32[2016]{0:T(1024)S(1)}, u32[]{:S(2)}, u32[]{:S(2)}) collective-permute-start(f32[2016]{0:T(1024)S(1)} %pad_maximum_fusion.5), channel_id=1, source_target_pairs={{0,2},{1,3},{2,0},{3,1},{4,6},{5,7},{6,4},{7,5},{8,10},{9,11},{10,... | collective-permute-start | bytes 24200 | tf_op jit(solution)/shard_map/ppermute | solution.py:638
  350.6 21.4 %collective-permute-start.17 = (bf16[144,1152]{1,0:T(8,128)(2,1)}, bf16[144,1152]{1,0:T(8,128)(2,1)S(1)}, u32[]{:S(2)}, u32[]{:S(2)}) collective-permute-start(bf16[144,1152]{1,0:T(8,128)(2,1)} %get-tuple-element.196), channel_id=1, source_target_pairs={{0,8},{4,12},{8,0},{12,4},{16,24},{20,28},{24,16},{28,20},{1,9},{5... | collective-permute-start | bytes 995336 | tf_op jit(solution)/shard_map/ppermute | solution.py:824
  362.7 9.3 %collective-permute-start.18 = (bf16[144,1152]{1,0:T(8,128)(2,1)}, bf16[144,1152]{1,0:T(8,128)(2,1)}, u32[]{:S(2)}, u32[]{:S(2)}) collective-permute-start(bf16[144,1152]{1,0:T(8,128)(2,1)} %get-tuple-element.198), channel_id=1, source_target_pairs={{0,16},{4,20},{8,24},{12,28},{16,0},{20,4},{24,8},{28,12},{1,17},{... | collective-permute-start | bytes 995336 | tf_op jit(solution)/shard_map/ppermute | solution.py:824
  375.2 31.8 %collective-permute-start.31 = (bf16[144,1152]{1,0:T(8,128)(2,1)S(1)}, bf16[144,1152]{1,0:T(8,128)(2,1)S(1)}, u32[]{:S(2)}, u32[]{:S(2)}) collective-permute-start(bf16[144,1152]{1,0:T(8,128)(2,1)S(1)} %shard_map.326), channel_id=1, source_target_pairs={{0,2},{1,3},{2,0},{3,1},{4,6},{5,7},{6,4},{7,5},{8,10},{9,11},{10,... | collective-permute-start | bytes 995336 | tf_op jit(solution)/shard_map/ppermute | solution.py:638
  384.6 22.4 %collective-permute-start.28 = (bf16[144,1152]{1,0:T(8,128)(2,1)}, bf16[144,1152]{1,0:T(8,128)(2,1)S(1)}, u32[]{:S(2)}, u32[]{:S(2)}) collective-permute-start(bf16[144,1152]{1,0:T(8,128)(2,1)} %copy-done.69), channel_id=1, source_target_pairs={{0,8},{4,12},{8,0},{12,4},{16,24},{20,28},{24,16},{28,20},{1,9},{5... | collective-permute-start | bytes 995336 | tf_op jit(solution)/shard_map/ppermute | solution.py:824
  386.1 20.9 %collective-permute-start.29 = (bf16[144,1152]{1,0:T(8,128)(2,1)}, bf16[144,1152]{1,0:T(8,128)(2,1)S(1)}, u32[]{:S(2)}, u32[]{:S(2)}) collective-permute-start(bf16[144,1152]{1,0:T(8,128)(2,1)} %copy-done.68), channel_id=1, source_target_pairs={{0,16},{4,20},{8,24},{12,28},{16,0},{20,4},{24,8},{28,12},{1,17},{... | collective-permute-start | bytes 995336 | tf_op jit(solution)/shard_map/ppermute | solution.py:824
  387.0 20.0 %collective-permute-start.30 = (bf16[144,1152]{1,0:T(8,128)(2,1)}, bf16[144,1152]{1,0:T(8,128)(2,1)S(1)}, u32[]{:S(2)}, u32[]{:S(2)}) collective-permute-start(bf16[144,1152]{1,0:T(8,128)(2,1)} %copy-done.67), channel_id=1, source_target_pairs={{0,24},{4,28},{8,16},{12,20},{16,8},{20,12},{24,0},{28,4},{1,25},{... | collective-permute-start | bytes 995336 | tf_op jit(solution)/shard_map/ppermute | solution.py:824
  408.3 11.7 %collective-permute-start.34 = (bf16[144,1152]{1,0:T(8,128)(2,1)S(1)}, bf16[144,1152]{1,0:T(8,128)(2,1)S(1)}, u32[]{:S(2)}, u32[]{:S(2)}) collective-permute-start(bf16[144,1152]{1,0:T(8,128)(2,1)S(1)} %shard_map.328.refs_0_), channel_id=1, source_target_pairs={{0,24},{4,28},{8,16},{12,20},{16,8},{20,12},{24,0},{28,4},{1,25},{... | collective-permute-start | bytes 995336 | tf_op jit(solution)/shard_map/ppermute | solution.py:824
  408.7 15.5 %collective-permute-start.33 = (bf16[144,1152]{1,0:T(8,128)(2,1)S(1)}, bf16[144,1152]{1,0:T(8,128)(2,1)S(1)}, u32[]{:S(2)}, u32[]{:S(2)}) collective-permute-start(bf16[144,1152]{1,0:T(8,128)(2,1)S(1)} %shard_map.328.refs_0_), channel_id=1, source_target_pairs={{0,16},{4,20},{8,24},{12,28},{16,0},{20,4},{24,8},{28,12},{1,17},{... | collective-permute-start | bytes 995336 | tf_op jit(solution)/shard_map/ppermute | solution.py:824
  410.3 14.0 %collective-permute-start.32 = (bf16[144,1152]{1,0:T(8,128)(2,1)S(1)}, bf16[144,1152]{1,0:T(8,128)(2,1)S(1)}, u32[]{:S(2)}, u32[]{:S(2)}) collective-permute-start(bf16[144,1152]{1,0:T(8,128)(2,1)S(1)} %shard_map.328.refs_0_), channel_id=1, source_target_pairs={{0,8},{4,12},{8,0},{12,4},{16,24},{20,28},{24,16},{28,20},{1,9},{5... | collective-permute-start | bytes 995336 | tf_op jit(solution)/shard_map/ppermute | solution.py:824
  415.4 15.4 %collective-permute-start.26 = (f32[5,1152]{1,0:T(8,128)S(1)}, f32[5,1152]{1,0:T(8,128)S(1)}, u32[]{:S(2)}, u32[]{:S(2)}) collective-permute-start(f32[5,1152]{1,0:T(8,128)S(1)} %convolution_bitcast_fusion), channel_id=1, source_target_pairs={{0,1},{1,0},{2,3},{3,2},{4,5},{5,4},{6,7},{7,6},{8,9},{9,8},{10,11... | collective-permute-start | bytes 69128 | tf_op jit(solution)/shard_map/ppermute | solution.py:1007
  424.4 11.9 %collective-permute-start.35 = (bf16[4,144,1152]{2,1,0:T(8,128)(2,1)S(1)}, bf16[4,144,1152]{2,1,0:T(8,128)(2,1)S(1)}, u32[]{:S(2)}, u32[]{:S(2)}) collective-permute-start(bf16[4,144,1152]{2,1,0:T(8,128)(2,1)S(1)} %shard_map.329.own_ref), channel_id=1, source_target_pairs={{0,4},{4,0},{8,12},{12,8},{16,20},{20,16},{24,28},{28,24},{1,5},{5... | collective-permute-start | bytes 3981320 | tf_op jit(solution)/shard_map/ppermute | solution.py:824
  (91 other events, 552.0 us)
Sparse Core Ops, SparseCore 0:
  46.0 31.6 all-gather.4
  86.7 40.7 all-gather.6
  221.3 81.5 reduce-scatter.1
  345.4 49.5 all-gather.8

commit v2 on v1

--- a/solution.py
+++ b/solution.py
@@ -146,13 +146,13 @@
     return kernel_call(
         qkv_kernel,
         jax.ShapeDtypeStruct((rows.shape[0], columns), bf16),
-        grid=(rows.shape[0] // BLOCK,),
+        grid=(2,),
         in_specs=[
-            pl.BlockSpec((BLOCK, rows.shape[1]), lambda index: (index, 0)),
+            pl.BlockSpec((rows.shape[0] // 2, rows.shape[1]), lambda index: (index, 0)),
             whole(pack),
             whole(bias),
         ],
-        out_specs=pl.BlockSpec((BLOCK, columns), lambda index: (index, 0)),
+        out_specs=pl.BlockSpec((rows.shape[0] // 2, columns), lambda index: (index, 0)),
     )(rows, pack, bias)
 
 
@@ -320,22 +320,39 @@
         d_branch_ref[...] = (mod_ref[5:6, :] * grad_ref[...].astype(f32)).astype(bf16)
 
     sums_ref[...] = jnp.zeros_like(sums_ref)
-    rows = x_ref.shape[0]
-    for start in range(0, rows, BLOCK):
+
+    def products(start, shard):
         block = slice(start, start + BLOCK)
-        d_mlp, branch = 0.0, 0.0
-        for shard in range(shard_count):
-            pre_act = dot(x_ref[block], up_refs[shard][...]) + bias_ref[shard].astype(f32)
-            hidden, slope = gelu_and_slope(pre_act)
-            d_pre = (dot_t(d_branch_ref[block], down_refs[shard][...]) * slope).astype(bf16)
-            hidden = hidden.astype(bf16)
-            hidden_ref[shard, block] = hidden
-            d_pre_ref[shard, block] = d_pre
-            sums_ref[shard : shard + 1] += jnp.sum(d_pre.astype(f32), axis=0, keepdims=True)
-            d_mlp = d_mlp + dot_t(d_pre, up_refs[shard][...])
-            branch = branch + dot(hidden, down_refs[shard][...])
-        d_mlp_scratch[block] += d_mlp
-        branch_scratch[block] += branch
+        pre_act = dot(x_ref[block], up_refs[shard][...]) + bias_ref[shard].astype(f32)
+        return pre_act, dot_t(d_branch_ref[block], down_refs[shard][...])
+
+    def activation(start, shard, pair):
+        block = slice(start, start + BLOCK)
+        pre_act, d_hidden = pair
+        hidden, slope = gelu_and_slope(pre_act)
+        hidden, d_pre = hidden.astype(bf16), (d_hidden * slope).astype(bf16)
+        hidden_ref[shard, block] = hidden
+        d_pre_ref[shard, block] = d_pre
+        sums_ref[shard : shard + 1] += jnp.sum(d_pre.astype(f32), axis=0, keepdims=True)
+        return hidden, d_pre
+
+    def add_sums(start, shard, pair):
+        block = slice(start, start + BLOCK)
+        hidden, d_pre = pair
+        d_mlp_scratch[block] += dot_t(d_pre, up_refs[shard][...])
+        branch_scratch[block] += dot(hidden, down_refs[shard][...])
+
+    units = [
+        (start, shard) for start in range(0, x_ref.shape[0], BLOCK) for shard in range(shard_count)
+    ]
+    begun, done = products(*units[0]), None
+    for at, unit in enumerate(units):
+        coming = products(*units[at + 1]) if at + 1 < len(units) else None
+        if done is not None:
+            add_sums(*units[at - 1], done)
+        done = activation(*unit, begun)
+        begun = coming
+    add_sums(*units[-1], done)
 
     @pl.when(pl.program_id(0) == pl.num_programs(0) - 1)
     def _():
@@ -682,7 +699,7 @@
 
     packs = [own_pack]
     packs += gathered(
-        [after(each, mod_part, token_rows[-1], *bias_packs[1:]) for each in attn_pieces]
+        [after(each, *mod_blocks[1:], token_rows[-1], *bias_packs[1:]) for each in attn_pieces]
     )
     qkv_biases = [pack[: 3 * local] for pack in bias_packs]
     up_biases = jnp.stack([pack[3 * local :] for pack in bias_packs]).reshape(slot_count, 1, -1)
@@ -796,7 +813,6 @@
             kept.append(result)
     arrived = [send_rows(d_mlp[block], block) for block in others]
     grad_mlp_part = mlp_gradients(mlp_rows, d_branch_two, hidden, d_pre, n_wide)
-    up_bias_sums = sum(bias_sums_up)[:slot_count]
 
     def d_middle_body(rows, vectors):
         token, branch, grad, *parts = [each.astype(f32) for each in rows]
@@ -947,6 +963,7 @@
     sent = [send_shard(each, index) for index, each in zip(other_shards, piece_sums)]
     mlp_total = add_arrays(mlp_sent[0], *(after(each, own_d_attn) for each in mlp_arrived))
 
+    middle_sums, out_sums = after(middle_sums, end_sums), after(out_sums, end_sums)
     own_sums = jnp.concatenate(
         [end_sums[0:2], middle_sums[0:3], out_sums[0:1], middle_sums[3:4], out_sums[1:2]]
     )
@@ -956,6 +973,9 @@
             own_sums, "narrow", [(at, at ^ bit) for at in range(n_narrow)]
         )
         bit *= 2
+    attn_bias_sums = [after(each, end_sums) for each in attn_bias_sums]
+    up_bias_sums = sum([after(each, end_sums) for each in bias_sums_up])
+    late_slot_clip = after(slot_clip, end_sums)
     shard_parts = [
         jnp.concatenate([attn_bias_sums[step].reshape(-1), up_bias_sums[step]])
         for step in range(slot_count)
@@ -975,7 +995,7 @@
     bias_sums = jnp.zeros((2, width), f32)
     shard_sum = jnp.zeros((3 * local + hidden_local,), f32)
     for step in range(slot_count):
-        source_clip = slot_clip[(slot + step) % slot_count]
+        source_clip = late_slot_clip[(slot + step) % slot_count]
         one_hot = (clip_ids == source_clip).astype(f32)
         columns = lax.dynamic_slice_in_dim(slot_sums[step][:6], narrow_index * local, local, 1)
         d_mod_clips = d_mod_clips + one_hot[:, None, None] * columns
@@ -1004,7 +1024,8 @@
     )
     bit = 1
     while bit < n_narrow:
-        d_silu = d_silu + lax.ppermute(d_silu, "narrow", [(at, at ^ bit) for at in range(n_narrow)])
+        flipped = lax.ppermute(d_silu, "narrow", [(at, at ^ bit) for at in range(n_narrow)])
+        d_silu = d_silu + (after(flipped, grad_up_weight) if bit == 1 else flipped)
         bit *= 2
     grad_condition = jax.vjp(jax.nn.silu, cond_float)[1](d_silu)[0]
     return (

time: 462 us -> 469 us (1.015)
  waiting for transfers between devices: 116 us -> 122 us
    ppermute x15, waiting for transfers between devices: 30.9 us -> 46.5 us  [wide_xor(): lax.ppermute(array, 'wide', [(at, at ^ mask) for at in range(n_wide)])]
    ppermute x1, waiting for transfers between devices: 4.73 us -> 0.01 us  [shards(): lax.ppermute(own_sums, 'narrow', [(at, at ^ bit) for at in range(n_narrow)])]
  transfers between devices with their start and end apart: 41 -> 41, of which waited for: 20 -> 19; matrix products, arithmetic and copies ran while one was open for 5% -> 5% of each run, Pallas kernels for 42% -> 42%
where the time goes in v2:
time: 469 us; the launch traced here: 460 us
  Pallas kernels  216 us (46%)
  waiting for transfers between devices  122 us (26%)
  starting transfers between devices  44.6 us (10%)
  local copies, waits for them, and re-layouts  41.9 us (9%)
  between operations  17.1 us (4%)
  matrix products  12.4 us (3%)
  other arithmetic  6.28 us (1%)
    ppermute x15, waiting for transfers between devices, wide_xor(): lax.ppermute(array, 'wide', [(at, at ^ mask) for at in range(n_wide)])  46.5 us
    pallas_call x4, Pallas kernels, attention_backward(): kernel_call(functools.partial(attention_backward_kernel, first_row, first...  45.8 us
    pallas_call x2, Pallas kernels, feed_forward(): kernel_call(functools.partial(feed_forward_kernel, sum_type, shard_count)...  44.5 us
    ppermute x4, waiting for transfers between devices, fetch_shard(): lax.ppermute(array, 'narrow', [((at + step * members) % n_narrow, at) for...  40.4 us
    pallas_call x9, Pallas kernels, row_call(): kernel_call(kernel, outs, grid=(rows // step_rows,), in_specs=[pl.BlockSp...  39.4 us
    unnamed x167, local copies, waits for them, and re-layouts  34.5 us
    pallas_call x6, Pallas kernels, attention_forward(): kernel_call(functools.partial(attention_forward_kernel, first_row), (jax....  23.5 us
    ppermute x5, waiting for transfers between devices, send_rows(): lax.ppermute(array, 'narrow', [(at, member_of(at, step)) for at in range(...  20.9 us
  transfers between devices with their start and end apart: 41, of which 19 were waited for; matrix products, arithmetic and copies ran while one was open for 5% of the time, Pallas kernels for 42%

profile of v2, /device:TPU:0, one launch (start us, length us, event | category | flops | bytes accessed | tf_op | source)
XLA Modules:
  0.0 460.3 jit_solution(18062665753659546167)
XLA Ops:
  9.3 4.1 collective-permute-start.4
  22.3 23.8 %collective-permute-done.5 = bf16[2016]{0:T(1024)(128)(2,1)S(1)} collective-permute-done((bf16[2016]{0:T(1024)(128)(2,1)S(1)}, bf16[2016]{0:T(1024)(128)(2,1)S(1)}, u32[]{:S(2)}, u32[]{:S(2)}) %collective-permute-start.5) | collective-permute-done | bytes 4064 | tf_op jit(solution)/shard_map/ppermute | solution.py:648
  62.8 5.6 %shard_map.298.qkv_ref.refs_1_ = bf16[1024,864]{1,0:T(8,128)(2,1)S(1)} custom-call(bf16[1024,1152]{1,0:T(8,128)(2,1)S(1)} %bitcast.39, bf16[1152,1152]{1,0:T(8,128)(2,1)} %copy-done, bf16[1,864]{1,0:T(2,128)(2,1)S(1)} %reshape.101.bias_ref), custom_call_target="tpu_custom_call" | custom-call | bytes 1024 | tf_op jit(solution)/shard_map/pallas_call | solution.py:146
  72.2 12.1 %collective-permute-done.6 = bf16[144,2304]{1,0:T(8,128)(2,1)S(1)} collective-permute-done((bf16[144,2304]{1,0:T(8,128)(2,1)}, bf16[144,2304]{1,0:T(8,128)(2,1)S(1)}, u32[]{:S(2)}, u32[]{:S(2)}) %collective-permute-start.6) | collective-permute-done | bytes 663584 | tf_op jit(solution)/shard_map/ppermute | solution.py:648
  90.7 5.1 %shard_map.300.qkv_ref.refs_1_ = bf16[1024,864]{1,0:T(8,128)(2,1)S(1)} custom-call(bf16[1024,1152]{1,0:T(8,128)(2,1)S(1)} %bitcast.42, bf16[1152,1152]{1,0:T(8,128)(2,1)} %all-gather.5.cloned.1.call-done.pack_ref.refs_4_.refs_3_.refs_6_, bf16[1,864]{1,0:T(2,128)(2,1)S(1)} %reshape.102.bias_ref), custom_call_target="tpu_custom_call" | custom-call | bytes 1024 | tf_op jit(solution)/shard_map/pallas_call | solution.py:146
  110.5 5.0 %shard_map.306 = (bf16[512,288]{1,0:T(8,128)(2,1)S(1)}, bf16[288,512]{1,0:T(8,128)(2,1)S(1)}, f32[4,512]{1,0:T(4,128)S(1)}) custom-call(s32[1]{0:T(128)} %dynamic_slice.45.patches_ref.refs_0_, bf16[1024,864]{1,0:T(8,128)(2,1)S(1)} %copy-done.3), custom_call_target="tpu_custom_call" | custom-call | bytes 1024 | tf_op jit(solution)/shard_map/pallas_call | solution.py:221
  115.5 5.9 %shard_map.307 = (bf16[512,288]{1,0:T(8,128)(2,1)S(1)}, bf16[288,512]{1,0:T(8,128)(2,1)S(1)}, f32[4,512]{1,0:T(4,128)S(1)}) custom-call(s32[1]{0:T(128)} %dynamic_slice.45.patches_ref.refs_0_, bf16[1024,864]{1,0:T(8,128)(2,1)S(1)} %shard_map.300.qkv_ref.refs_1_), custom_call_target="tpu_custom_call" | custom-call | bytes 1024 | tf_op jit(solution)/shard_map/pallas_call | solution.py:221
  126.9 11.7 %collective-permute-done.8 = bf16[256,1152]{1,0:T(8,128)(2,1)S(1)} collective-permute-done((bf16[256,1152]{1,0:T(8,128)(2,1)S(1)}, bf16[256,1152]{1,0:T(8,128)(2,1)S(1)}, u32[]{:S(2)}, u32[]{:S(2)}) %collective-permute-start.8) | collective-permute-done | bytes 589856 | tf_op jit(solution)/shard_map/ppermute | solution.py:643
  143.2 22.7 %shard_map.310 = (bf16[2,512,1152]{2,1,0:T(8,128)(2,1)S(1)}, bf16[2,512,1152]{2,1,0:T(8,128)(2,1)}, bf16[512,1152]{1,0:T(8,128)(2,1)S(1)}, f32[512,1152]{1,0:T(8...) custom-call(bf16[512,1152]{1,0:T(8,128)(2,1)S(1)} %get-tuple-element.144.refs_0_, bf16[512,1152]{1,0:T(8,128)(2,1)} %refs_2_.3, ...), custom_call_target="tpu_custom_call" | custom-call | bytes 1024 | tf_op jit(solution)/shard_map/pallas_call | solution.py:376
  169.8 21.9 %shard_map.311 = (bf16[2,512,1152]{2,1,0:T(8,128)(2,1)}, bf16[2,512,1152]{2,1,0:T(8,128)(2,1)}, bf16[512,1152]{1,0:T(8,128)(2,1)S(1)}, bf16[512,1152]{1,0:T(8,12...) custom-call(bf16[512,1152]{1,0:T(8,128)(2,1)S(1)} %collective-permute-done.10.refs_0_.refs_1_, ...), custom_call_target="tpu_custom_call" | custom-call | bytes 1024 | tf_op jit(solution)/shard_map/pallas_call | solution.py:376
  192.9 17.1 %shard_map.312 = bf16[8,4,144,1152]{3,2,1,0:T(8,128)(2,1)} custom-call(bf16[512,1152]{1,0:T(8,128)(2,1)S(1)} %get-tuple-element.144.refs_0_, bf16[512,1152]{1,0:T(8,128)(2,1)S(1)} %collective-permute-done.10.refs_0_.refs_1_, bf16[512,1152]{1,0:T(8,128)(2,1)S(1)} %get-tuple-element.151.refs_2_, bf16[512,1152]{1,0:T(8,128)(2,1)S(1)} %get-tuple-element.152.refs_3_, ...), custom_call_target="tpu_custom_call" | custom-call | bytes 1024 | tf_op jit(solution)/shard_map/pallas_call | solution.py:428
  210.0 8.7 %collective-permute-done.11.refs_4_ = bf16[512,1152]{1,0:T(8,128)(2,1)} collective-permute-done((bf16[512,1152]{1,0:T(8,128)(2,1)}, bf16[512,1152]{1,0:T(8,128)(2,1)}, u32[]{:S(2)}, u32[]{:S(2)}) %collective-permute-start.11) | collective-permute-done | bytes 1179680 | tf_op jit(solution)/shard_map/ppermute | solution.py:643
  218.8 6.1 %shard_map.313 = (bf16[512,1152]{1,0:T(8,128)(2,1)}, f32[512,1152]{1,0:T(8,128)}, f32[8,1152]{1,0:T(8,128)S(1)}) custom-call(bf16[512,1152]{1,0:T(8,128)(2,1)} %refs_0_.9, f32[512,1152]{1,0:T(8,128)} %copy-done.9, bf16[512,1152]{1,0:T(8,128)(2,1)} %refs_2_.3, f32[512,1152]{1,0:T(8,128)} %get-tuple-element.147.refs_3_, ...), custom_call_target="tpu_custom_call" | custom-call | bytes 1024 | tf_op jit(solution)/shard_map/pallas_call | solution.py:103
  226.5 11.9 %shard_map.314 = (bf16[512,288]{1,0:T(8,128)(2,1)S(1)}, bf16[288,512]{1,0:T(8,128)(2,1)S(1)}, f32[576,1024]{1,0:T(8,128)S(1)}) custom-call(s32[1]{0:T(128)} %dynamic_slice.45.patches_ref.refs_0_, bf16[1024,864]{1,0:T(8,128)(2,1)S(1)} %copy-done.4, bf16[512,1152]{1,0:T(8,128)(2,1)} %get-tuple-element.158.refs_2_.refs_5_, bf16[1152,1152]{1,0:T(8,128)(2,1)} %copy-done, ...), custom_call_target="tpu_custom_call" | custom-call | bytes 1024 | tf_op jit(solution)/shard_map/pallas_call | solution.py:296
  241.3 10.6 %shard_map.315 = (bf16[512,288]{1,0:T(8,128)(2,1)S(1)}, bf16[288,512]{1,0:T(8,128)(2,1)S(1)}, f32[576,1024]{1,0:T(8,128)S(1)}) custom-call(s32[1]{0:T(128)} %dynamic_slice.45.patches_ref.refs_0_, bf16[1024,864]{1,0:T(8,128)(2,1)S(1)} %copy-done.6, bf16[512,1152]{1,0:T(8,128)(2,1)} %get-tuple-element.158.refs_2_.refs_5_, ...), custom_call_target="tpu_custom_call" | custom-call | bytes 1024 | tf_op jit(solution)/shard_map/pallas_call | solution.py:296
  254.2 11.7 %shard_map.316 = (bf16[512,288]{1,0:T(8,128)(2,1)S(1)}, bf16[288,512]{1,0:T(8,128)(2,1)S(1)}, bf16[1024,576]{1,0:T(8,128)(2,1)S(1)}, bf16[576,1024]{1,0:T(8,128)(2,1)S(1)}) custom-call(s32[1]{0:T(128)} %dynamic_slice.45.patches_ref.refs_0_, bf16[1024,864]{1,0:T(8,128)(2,1)S(1)} %copy-done.6, bf16[512,1152]{1,0:T(8,128)(2,1)S(1)} %collective-permute-done.12.refs_2_.refs_6_, ...), custom_call_target="tpu_custom_call" | custom-call | bytes 1024 | tf_op jit(solution)/shard_map/pallas_call | solution.py:296
  267.7 6.9 %shard_map.317 = (bf16[4,144,1152]{2,1,0:T(8,128)(2,1)}, bf16[4,144,1152]{2,1,0:T(8,128)(2,1)}, f32[864,1]{1,0:T(8,128)S(1)}) custom-call(s32[1]{0:T(128)} %bitcast.8.refs_0_.core_ref, bf16[1024,1152]{1,0:T(8,128)(2,1)} %bitcast.40, bf16[576,1024]{1,0:T(8,128)(2,1)S(1)} %get-tuple-element.166.refs_2_, bf16[288,512]{1,0:T(8,128)(2,1)S(1)} %get-tuple-element.167.refs_3_, ...), custom_call_target="tpu_custom_call" | custom-call | bytes 1024 | tf_op jit(solution)/shard_map/pallas_call | solution.py:480
  275.9 11.6 %shard_map.318 = (bf16[512,288]{1,0:T(8,128)(2,1)S(1)}, bf16[288,512]{1,0:T(8,128)(2,1)S(1)}, bf16[1024,576]{1,0:T(8,128)(2,1)S(1)}, bf16[576,1024]{1,0:T(8,128)(2,1)S(1)}) custom-call(s32[1]{0:T(128)} %dynamic_slice.45.patches_ref.refs_0_, bf16[1024,864]{1,0:T(8,128)(2,1)S(1)} %copy-done.4, bf16[512,1152]{1,0:T(8,128)(2,1)S(1)} %collective-permute-done.12.refs_2_.refs_6_, ...), custom_call_target="tpu_custom_call" | custom-call | bytes 1024 | tf_op jit(solution)/shard_map/pallas_call | solution.py:296
  291.1 8.6 %reduce-scatter.2.cloned.1.call-done = bf16[1,4,144,1152]{3,2,1,0:T(8,128)(2,1)} async-done(((bf16[8,4,144,1152]{3,2,1,0:T(8,128)(2,1)}), bf16[1,4,144,1152]{3,2,1,0:T(8,128)(2,1)}) %reduce-scatter.2.cloned.1.call-update) | async-done | bytes 1327120 | tf_op jit(solution)/shard_map/reduce_scatter | solution.py:831
  310.4 7.0 %shard_map.321 = (bf16[4,144,1152]{2,1,0:T(8,128)(2,1)}, bf16[4,144,1152]{2,1,0:T(8,128)(2,1)}, f32[864,1]{1,0:T(8,128)S(1)}) custom-call(s32[1]{0:T(128)} %bitcast.8.refs_0_.core_ref, bf16[1024,1152]{1,0:T(8,128)(2,1)} %bitcast.41, bf16[576,1024]{1,0:T(8,128)(2,1)S(1)} %copy-done.29, bf16[288,512]{1,0:T(8,128)(2,1)S(1)} %copy-done.49, ...), custom_call_target="tpu_custom_call" | custom-call | bytes 1024 | tf_op jit(solution)/shard_map/pallas_call | solution.py:480
  318.2 6.5 %shard_map.322 = bf16[512,1152]{1,0:T(8,128)(2,1)S(1)} custom-call(bf16[512,288]{1,0:T(8,128)(2,1)S(1)} %copy-done.35, bf16[1024,576]{1,0:T(8,128)(2,1)S(1)} %copy-done.17, bf16[512,288]{1,0:T(8,128)(2,1)S(1)} %copy-done.33, bf16[1024,576]{1,0:T(8,128)(2,1)S(1)} %copy-done.15, f32[1,1152]{1,0:T(1,128)S(1)} %broadcast_in_dim.16.refs_2_.refs_4_, ...), custom_call_target="tpu_custom_call" | custom-call | bytes 1024 | tf_op jit(solution)/shard_map/pallas_call | solution.py:103
  325.8 4.1 shard_map.323
  329.9 6.2 %shard_map.324.refs_2_ = f32[512,1152]{1,0:T(8,128)S(1)} custom-call(bf16[512,288]{1,0:T(8,128)(2,1)S(1)} %copy-done.37, bf16[1024,576]{1,0:T(8,128)(2,1)S(1)} %copy-done.17, bf16[512,288]{1,0:T(8,128)(2,1)S(1)} %copy-done.39, bf16[1024,576]{1,0:T(8,128)(2,1)S(1)} %copy-done.15, f32[1,1152]{1,0:T(1,128)S(1)} %broadcast_in_dim.16.refs_2_.refs_4_, ...), custom_call_target="tpu_custom_call" | custom-call | bytes 1024 | tf_op jit(solution)/shard_map/pallas_call | solution.py:103
  344.7 11.2 %collective-permute-done.17.refs_1_ = bf16[144,1152]{1,0:T(8,128)(2,1)S(1)} collective-permute-done((bf16[144,1152]{1,0:T(8,128)(2,1)}, bf16[144,1152]{1,0:T(8,128)(2,1)S(1)}, u32[]{:S(2)}, u32[]{:S(2)}) %collective-permute-start.17) | collective-permute-done | bytes 331808 | tf_op jit(solution)/shard_map/ppermute | solution.py:840
  359.5 7.0 %collective-permute-done.19.refs_3_ = bf16[144,1152]{1,0:T(8,128)(2,1)} collective-permute-done((bf16[144,1152]{1,0:T(8,128)(2,1)}, bf16[144,1152]{1,0:T(8,128)(2,1)}, u32[]{:S(2)}, u32[]{:S(2)}) %collective-permute-start.19) | collective-permute-done | bytes 331808 | tf_op jit(solution)/shard_map/ppermute | solution.py:840
  372.9 5.1 %shard_map.327 = (f32[512,1152]{1,0:T(8,128)}, f32[8,1152]{1,0:T(8,128)S(1)}) custom-call(bf16[512,1152]{1,0:T(8,128)(2,1)} %refs_0_.9, f32[512,1152]{1,0:T(8,128)S(1)} %copy-done.19, f32[512,1152]{1,0:T(8,128)} %copy-done.11, bf16[512,1152]{1,0:T(8,128)(2,1)} %collective-permute-done.15.refs_3_, f32[6,1152]{1,0:T(8,128)S(1)} %reshape.99.refs_2_.refs_3_.refs_5_.refs_4_), custom_call_target="tpu_custom_call" | custom-call | bytes 1024 | tf_op jit(solution)/shard_map/pallas_call | solution.py:103
  389.0 4.4 collective-permute-done.21
  395.7 5.1 %collective-permute-done.31.refs_3_ = bf16[144,1152]{1,0:T(8,128)(2,1)S(1)} collective-permute-done((bf16[144,1152]{1,0:T(8,128)(2,1)}, bf16[144,1152]{1,0:T(8,128)(2,1)S(1)}, u32[]{:S(2)}, u32[]{:S(2)}) %collective-permute-start.31) | collective-permute-done | bytes 331808 | tf_op jit(solution)/shard_map/ppermute | solution.py:840
  406.7 7.1 %collective-permute-done.33.refs_1_ = bf16[144,1152]{1,0:T(8,128)(2,1)S(1)} collective-permute-done((bf16[144,1152]{1,0:T(8,128)(2,1)S(1)}, bf16[144,1152]{1,0:T(8,128)(2,1)S(1)}, u32[]{:S(2)}, u32[]{:S(2)}) %collective-permute-start.33) | collective-permute-done | bytes 331808 | tf_op jit(solution)/shard_map/ppermute | solution.py:840
  413.8 4.4 collective-permute-done.34.refs_2_
  431.9 5.5 %fusion = f32[1152,6,288]{0,2,1:T(8,128)} fusion(f32[5,6,288]{2,1,0:T(8,128)S(1)} %reshape.112, bf16[5,1152]{1,0:T(8,128)(2,1)S(1)} %copy-done.73), kind=kOutput, calls=%fused_computation.6 | convolution fusion | flops 119473920 | bytes 8008704 | tf_op jit(solution)/shard_map/cd,cke->dke/dot_general | solution.py:1020
  440.6 4.8 %shard_map.329 = (f32[1152,1152]{1,0:T(8,128)}, f32[1152,1152]{1,0:T(8,128)}) custom-call(bf16[8,2,144,1152]{3,2,1,0:T(8,128)(2,1)S(1)} %bitcast.43), custom_call_target="tpu_custom_call" | custom-call | bytes 1024 | tf_op jit(solution)/shard_map/pallas_call | solution.py:587
  (327 shorter events, 153.6 us)
Async XLA Ops:
  7.2 81.8 %all-gather.5.cloned.1.call-start = ((), (), s32[]{:S(2)}) async-start(), calls=%async_computation.1 | async-start | bytes 2985984 | tf_op jit(solution)/shard_map/all_gather | solution.py:669
  9.3 42.4 %collective-permute-start.4 = (bf16[144,1152]{1,0:T(8,128)(2,1)S(1)}, bf16[144,1152]{1,0:T(8,128)(2,1)S(1)}, u32[]{:S(2)}, u32[]{:S(2)}) collective-permute-start(bf16[144,1152]{1,0:T(8,128)(2,1)S(1)} %constant_dynamic-slice_fusion.8), channel_id=1, source_target_pairs={{2,0},{3,1},{0,2},{1,3},{6,4},{7,5},{4,6},{5,7},{10,8},{11,9},{8,1... | collective-permute-start | bytes 995336 | tf_op jit(solution)/shard_map/ppermute | solution.py:648
  13.4 38.3 %collective-permute-start = (bf16[512,1152]{1,0:T(8,128)(2,1)}, bf16[512,1152]{1,0:T(8,128)(2,1)}, u32[]{:S(2)}, u32[]{:S(2)}) collective-permute-start(bf16[512,1152]{1,0:T(8,128)(2,1)} %refs_0_.9), channel_id=1, source_target_pairs={{1,0},{0,1},{3,2},{2,3},{5,4},{4,5},{7,6},{6,7},{9,8},{8,9},{11,10... | collective-permute-start | bytes 3538952 | tf_op jit(solution)/shard_map/ppermute | solution.py:638
  15.1 31.1 %collective-permute-start.5 = (bf16[2016]{0:T(1024)(128)(2,1)S(1)}, bf16[2016]{0:T(1024)(128)(2,1)S(1)}, u32[]{:S(2)}, u32[]{:S(2)}) collective-permute-start(bf16[2016]{0:T(1024)(128)(2,1)S(1)} %concatenate.41), channel_id=1, source_target_pairs={{2,0},{3,1},{0,2},{1,3},{6,4},{7,5},{4,6},{5,7},{10,8},{11,9},{8,1... | collective-permute-start | bytes 12104 | tf_op jit(solution)/shard_map/ppermute | solution.py:648
  19.6 28.9 %collective-permute-start.1 = (f32[6,288]{1,0:T(8,128)S(1)}, f32[6,288]{1,0:T(8,128)S(1)}, u32[]{:S(2)}, u32[]{:S(2)}) collective-permute-start(f32[6,288]{1,0:T(8,128)S(1)} %bitcast.50), channel_id=1, source_target_pairs={{0,3},{1,0},{2,1},{3,2},{4,7},{5,4},{6,5},{7,6},{8,11},{9,8},{10,9... | collective-permute-start | bytes 20744 | tf_op jit(solution)/shard_map/ppermute | solution.py:693
  22.1 26.3 %collective-permute-start.2 = (f32[6,288]{1,0:T(8,128)S(1)}, f32[6,288]{1,0:T(8,128)S(1)}, u32[]{:S(2)}, u32[]{:S(2)}) collective-permute-start(f32[6,288]{1,0:T(8,128)S(1)} %bitcast.51), channel_id=1, source_target_pairs={{0,2},{1,3},{2,0},{3,1},{4,6},{5,7},{6,4},{7,5},{8,10},{9,11},{10,... | collective-permute-start | bytes 20744 | tf_op jit(solution)/shard_map/ppermute | solution.py:693
  52.4 90.8 %all-gather.7.cloned.1.call-start = ((), (), s32[]{:S(2)}) async-start(), calls=%async_computation.2 | async-start | bytes 5971968 | tf_op jit(solution)/shard_map/all_gather | solution.py:669
  54.8 29.5 %collective-permute-start.6 = (bf16[144,2304]{1,0:T(8,128)(2,1)}, bf16[144,2304]{1,0:T(8,128)(2,1)S(1)}, u32[]{:S(2)}, u32[]{:S(2)}) collective-permute-start(bf16[144,2304]{1,0:T(8,128)(2,1)} %pad_maximum_fusion.2), channel_id=1, source_target_pairs={{2,0},{3,1},{0,2},{1,3},{6,4},{7,5},{4,6},{5,7},{10,8},{11,9},{8,1... | collective-permute-start | bytes 1990664 | tf_op jit(solution)/shard_map/ppermute | solution.py:648
  85.1 214.6 %reduce-scatter.2.cloned.1.call-start = ((), (), s32[]{:S(2)}) async-start(), calls=%async_computation.3 | async-start | bytes 11943936 | tf_op jit(solution)/shard_map/reduce_scatter | solution.py:831
  85.2 30.3 %collective-permute-start.7 = (bf16[512,1152]{1,0:T(8,128)(2,1)}, bf16[512,1152]{1,0:T(8,128)(2,1)S(1)}, u32[]{:S(2)}, u32[]{:S(2)}) collective-permute-start(bf16[512,1152]{1,0:T(8,128)(2,1)} %refs_2_.3), channel_id=1, source_target_pairs={{1,0},{0,1},{3,2},{2,3},{5,4},{4,5},{7,6},{6,7},{9,8},{8,9},{11,10... | collective-permute-start | bytes 3538952 | tf_op jit(solution)/shard_map/ppermute | solution.py:638
  108.3 18.6 %collective-permute-start.9 = (bf16[256,1152]{1,0:T(8,128)(2,1)S(1)}, bf16[256,1152]{1,0:T(8,128)(2,1)S(1)}, u32[]{:S(2)}, u32[]{:S(2)}) collective-permute-start(bf16[256,1152]{1,0:T(8,128)(2,1)S(1)} %shard_map.305), channel_id=1, source_target_pairs={{0,1},{1,0},{2,3},{3,2},{4,5},{5,4},{6,7},{7,6},{8,9},{9,8},{10,11... | collective-permute-start | bytes 1769480 | tf_op jit(solution)/shard_map/ppermute | solution.py:643
  110.4 28.2 %collective-permute-start.8 = (bf16[256,1152]{1,0:T(8,128)(2,1)S(1)}, bf16[256,1152]{1,0:T(8,128)(2,1)S(1)}, u32[]{:S(2)}, u32[]{:S(2)}) collective-permute-start(bf16[256,1152]{1,0:T(8,128)(2,1)S(1)} %shard_map.303), channel_id=1, source_target_pairs={{0,1},{1,0},{2,3},{3,2},{4,5},{5,4},{6,7},{7,6},{8,9},{9,8},{10,11... | collective-permute-start | bytes 1769480 | tf_op jit(solution)/shard_map/ppermute | solution.py:643
  142.8 27.0 %collective-permute-start.10 = (bf16[512,1152]{1,0:T(8,128)(2,1)S(1)}, bf16[512,1152]{1,0:T(8,128)(2,1)S(1)}, u32[]{:S(2)}, u32[]{:S(2)}) collective-permute-start(bf16[512,1152]{1,0:T(8,128)(2,1)S(1)} %get-tuple-element.144.refs_0_), channel_id=1, source_target_pairs={{1,0},{0,1},{3,2},{2,3},{5,4},{4,5},{7,6},{6,7},{9,8},{8,9},{11,10... | collective-permute-start | bytes 3538952 | tf_op jit(solution)/shard_map/ppermute | solution.py:638
  192.3 26.4 %collective-permute-start.11 = (bf16[512,1152]{1,0:T(8,128)(2,1)}, bf16[512,1152]{1,0:T(8,128)(2,1)}, u32[]{:S(2)}, u32[]{:S(2)}) collective-permute-start(bf16[512,1152]{1,0:T(8,128)(2,1)} %get-tuple-element.150), channel_id=1, source_target_pairs={{0,1},{1,0},{2,3},{3,2},{4,5},{5,4},{6,7},{7,6},{8,9},{9,8},{10,11... | collective-permute-start | bytes 3538952 | tf_op jit(solution)/shard_map/ppermute | solution.py:643
  218.8 219.4 %all-gather.9.cloned.1.call-start = ((), (), s32[]{:S(2)}) async-start(), calls=%async_computation.4 | async-start | bytes 5971968 | tf_op jit(solution)/shard_map/all_gather | solution.py:987
  225.6 28.6 %collective-permute-start.12 = (bf16[512,1152]{1,0:T(8,128)(2,1)}, bf16[512,1152]{1,0:T(8,128)(2,1)S(1)}, u32[]{:S(2)}, u32[]{:S(2)}) collective-permute-start(bf16[512,1152]{1,0:T(8,128)(2,1)} %get-tuple-element.158.refs_2_.refs_5_), channel_id=1, source_target_pairs={{1,0},{0,1},{3,2},{2,3},{5,4},{4,5},{7,6},{6,7},{9,8},{8,9},{11,10... | collective-permute-start | bytes 3538952 | tf_op jit(solution)/shard_map/ppermute | solution.py:638
  274.6 30.4 %collective-permute-start.14 = (bf16[4,144,1152]{2,1,0:T(8,128)(2,1)}, bf16[4,144,1152]{2,1,0:T(8,128)(2,1)}, u32[]{:S(2)}, u32[]{:S(2)}) collective-permute-start(bf16[4,144,1152]{2,1,0:T(8,128)(2,1)} %get-tuple-element.183), channel_id=1, source_target_pairs={{0,4},{4,0},{8,12},{12,8},{16,20},{20,16},{24,28},{28,24},{1,5},{5... | collective-permute-start | bytes 3981320 | tf_op jit(solution)/shard_map/ppermute | solution.py:840
  274.6 51.1 %collective-permute-start.13 = (bf16[512,1152]{1,0:T(8,128)(2,1)}, bf16[512,1152]{1,0:T(8,128)(2,1)}, u32[]{:S(2)}, u32[]{:S(2)}) collective-permute-start(bf16[512,1152]{1,0:T(8,128)(2,1)} %get-tuple-element.174), channel_id=1, source_target_pairs={{0,1},{1,0},{2,3},{3,2},{4,5},{5,4},{6,7},{7,6},{8,9},{9,8},{10,11... | collective-permute-start | bytes 3538952 | tf_op jit(solution)/shard_map/ppermute | solution.py:643
  302.0 35.5 %collective-permute-start.27 = (bf16[2,144,1152]{2,1,0:T(8,128)(2,1)}, bf16[2,144,1152]{2,1,0:T(8,128)(2,1)}, u32[]{:S(2)}, u32[]{:S(2)}) collective-permute-start(bf16[2,144,1152]{2,1,0:T(8,128)(2,1)} %get-tuple-element.182), channel_id=1, source_target_pairs={{0,2},{1,3},{2,0},{3,1},{4,6},{5,7},{6,4},{7,5},{8,10},{9,11},{10,... | collective-permute-start | bytes 1990664 | tf_op jit(solution)/shard_map/ppermute | solution.py:655
  339.6 30.2 %collective-permute-start.16 = (bf16[4,144,1152]{2,1,0:T(8,128)(2,1)}, bf16[4,144,1152]{2,1,0:T(8,128)(2,1)}, u32[]{:S(2)}, u32[]{:S(2)}) collective-permute-start(bf16[4,144,1152]{2,1,0:T(8,128)(2,1)} %get-tuple-element.201), channel_id=1, source_target_pairs={{0,4},{4,0},{8,12},{12,8},{16,20},{20,16},{24,28},{28,24},{1,5},{5... | collective-permute-start | bytes 3981320 | tf_op jit(solution)/shard_map/ppermute | solution.py:840
  339.7 33.2 %collective-permute-start.15 = (bf16[512,1152]{1,0:T(8,128)(2,1)}, bf16[512,1152]{1,0:T(8,128)(2,1)}, u32[]{:S(2)}, u32[]{:S(2)}) collective-permute-start(bf16[512,1152]{1,0:T(8,128)(2,1)} %copy-done.25), channel_id=1, source_target_pairs={{0,1},{1,0},{2,3},{3,2},{4,5},{5,4},{6,7},{7,6},{8,9},{9,8},{10,11... | collective-permute-start | bytes 3538952 | tf_op jit(solution)/shard_map/ppermute | solution.py:643
  341.2 14.7 %collective-permute-start.17 = (bf16[144,1152]{1,0:T(8,128)(2,1)}, bf16[144,1152]{1,0:T(8,128)(2,1)S(1)}, u32[]{:S(2)}, u32[]{:S(2)}) collective-permute-start(bf16[144,1152]{1,0:T(8,128)(2,1)} %get-tuple-element.204), channel_id=1, source_target_pairs={{0,8},{4,12},{8,0},{12,4},{16,24},{20,28},{24,16},{28,20},{1,9},{5... | collective-permute-start | bytes 995336 | tf_op jit(solution)/shard_map/ppermute | solution.py:840
  342.6 16.9 %collective-permute-start.18 = (bf16[144,1152]{1,0:T(8,128)(2,1)}, bf16[144,1152]{1,0:T(8,128)(2,1)S(1)}, u32[]{:S(2)}, u32[]{:S(2)}) collective-permute-start(bf16[144,1152]{1,0:T(8,128)(2,1)} %copy-done.66), channel_id=1, source_target_pairs={{0,16},{4,20},{8,24},{12,28},{16,0},{20,4},{24,8},{28,12},{1,17},{... | collective-permute-start | bytes 995336 | tf_op jit(solution)/shard_map/ppermute | solution.py:840
  343.3 23.2 %collective-permute-start.19 = (bf16[144,1152]{1,0:T(8,128)(2,1)}, bf16[144,1152]{1,0:T(8,128)(2,1)}, u32[]{:S(2)}, u32[]{:S(2)}) collective-permute-start(bf16[144,1152]{1,0:T(8,128)(2,1)} %copy-done.65), channel_id=1, source_target_pairs={{0,24},{4,28},{8,16},{12,20},{16,8},{20,12},{24,0},{28,4},{1,25},{... | collective-permute-start | bytes 995336 | tf_op jit(solution)/shard_map/ppermute | solution.py:840
  369.3 24.4 %collective-permute-start.32 = (bf16[144,1152]{1,0:T(8,128)(2,1)}, bf16[144,1152]{1,0:T(8,128)(2,1)}, u32[]{:S(2)}, u32[]{:S(2)}) collective-permute-start(bf16[144,1152]{1,0:T(8,128)(2,1)} %shard_map.326), channel_id=1, source_target_pairs={{0,2},{1,3},{2,0},{3,1},{4,6},{5,7},{6,4},{7,5},{8,10},{9,11},{10,... | collective-permute-start | bytes 995336 | tf_op jit(solution)/shard_map/ppermute | solution.py:655
  384.7 11.0 %collective-permute-start.29 = (bf16[144,1152]{1,0:T(8,128)(2,1)}, bf16[144,1152]{1,0:T(8,128)(2,1)S(1)}, u32[]{:S(2)}, u32[]{:S(2)}) collective-permute-start(bf16[144,1152]{1,0:T(8,128)(2,1)} %copy-done.69), channel_id=1, source_target_pairs={{0,8},{4,12},{8,0},{12,4},{16,24},{20,28},{24,16},{28,20},{1,9},{5... | collective-permute-start | bytes 995336 | tf_op jit(solution)/shard_map/ppermute | solution.py:840
  387.0 13.9 %collective-permute-start.31 = (bf16[144,1152]{1,0:T(8,128)(2,1)}, bf16[144,1152]{1,0:T(8,128)(2,1)S(1)}, u32[]{:S(2)}, u32[]{:S(2)}) collective-permute-start(bf16[144,1152]{1,0:T(8,128)(2,1)} %copy-done.67), channel_id=1, source_target_pairs={{0,24},{4,28},{8,16},{12,20},{16,8},{20,12},{24,0},{28,4},{1,25},{... | collective-permute-start | bytes 995336 | tf_op jit(solution)/shard_map/ppermute | solution.py:840
  404.3 13.9 %collective-permute-start.34 = (bf16[144,1152]{1,0:T(8,128)(2,1)S(1)}, bf16[144,1152]{1,0:T(8,128)(2,1)S(1)}, u32[]{:S(2)}, u32[]{:S(2)}) collective-permute-start(bf16[144,1152]{1,0:T(8,128)(2,1)S(1)} %shard_map.330.refs_0_), channel_id=1, source_target_pairs={{0,16},{4,20},{8,24},{12,28},{16,0},{20,4},{24,8},{28,12},{1,17},{... | collective-permute-start | bytes 995336 | tf_op jit(solution)/shard_map/ppermute | solution.py:840
  404.8 13.4 %collective-permute-start.35 = (bf16[144,1152]{1,0:T(8,128)(2,1)S(1)}, bf16[144,1152]{1,0:T(8,128)(2,1)S(1)}, u32[]{:S(2)}, u32[]{:S(2)}) collective-permute-start(bf16[144,1152]{1,0:T(8,128)(2,1)S(1)} %shard_map.330.refs_0_), channel_id=1, source_target_pairs={{0,24},{4,28},{8,16},{12,20},{16,8},{20,12},{24,0},{28,4},{1,25},{... | collective-permute-start | bytes 995336 | tf_op jit(solution)/shard_map/ppermute | solution.py:840
  406.7 11.8 %collective-permute-start.23 = (f32[12960]{0:T(1024)S(1)}, f32[12960]{0:T(1024)S(1)}, u32[]{:S(2)}, u32[]{:S(2)}) collective-permute-start(f32[12960]{0:T(1024)S(1)} %concatenate.49), channel_id=1, source_target_pairs={{0,4},{4,0},{8,12},{12,8},{16,20},{20,16},{24,28},{28,24},{1,5},{5... | collective-permute-start | bytes 155528 | tf_op jit(solution)/shard_map/ppermute | solution.py:840
  418.3 32.0 %collective-permute-start.36 = (bf16[4,144,1152]{2,1,0:T(8,128)(2,1)S(1)}, bf16[4,144,1152]{2,1,0:T(8,128)(2,1)S(1)}, u32[]{:S(2)}, u32[]{:S(2)}) collective-permute-start(bf16[4,144,1152]{2,1,0:T(8,128)(2,1)S(1)} %shard_map.331.own_ref), channel_id=1, source_target_pairs={{0,4},{4,0},{8,12},{12,8},{16,20},{20,16},{24,28},{28,24},{1,5},{5... | collective-permute-start | bytes 3981320 | tf_op jit(solution)/shard_map/ppermute | solution.py:840
  430.5 15.0 %collective-permute-start.26 = (f32[5,1152]{1,0:T(8,128)S(1)}, f32[5,1152]{1,0:T(8,128)S(1)}, u32[]{:S(2)}, u32[]{:S(2)}) collective-permute-start(f32[5,1152]{1,0:T(8,128)S(1)} %convolution_bitcast_fusion), channel_id=1, source_target_pairs={{0,1},{1,0},{2,3},{3,2},{4,5},{5,4},{6,7},{7,6},{8,9},{9,8},{10,11... | collective-permute-start | bytes 69128 | tf_op jit(solution)/shard_map/ppermute | solution.py:1027
  (91 other events, 565.1 us)
Sparse Core Ops, SparseCore 0:
  52.5 29.4 all-gather.4
  85.2 40.6 all-gather.6
  218.9 80.7 reduce-scatter.1
  339.7 47.7 all-gather.8
